TPU v7x, 128 devices: a whole 4x4x4 slice. The times are simulated.
128 devices in a mesh: panel: 4 (over x_lo, core), grp: 32 (over y, x_hi, z).
Axes of the slice: x: 4 (x_hi: 2, x_lo: 2; x = x_hi * 2 + x_lo), y: 4, z: 4, core: 2. Of those that a mesh axis runs over, the one named last changes fastest.
Arguments:
- b_blocks: bfloat16 [16384, 2048], P('grp', 'panel'), may hold values from -6 to 6
- w_store: bfloat16 [16384, 16384], P('grp', 'panel'), may hold values from -0.046875 to 0.046875
- owner: int32 [4], replicated, may hold values from 0 to 3, each once
- trials: bfloat16 [2048, 64], P(('panel', 'grp')), may hold values from -6 to 6
- eps_occ: float32 [128], replicated, may hold values from -3 to -0.5
- eps_virt: float32 [2048], replicated, may hold values from 0.5 to 3
- slab_first: int32 [1], replicated, may hold values from 0 to 127
Outputs:
- kernel_blocks: bfloat16 [2048, 16384], P(('panel', 'grp'))
- sigma: float32 [2048, 64], P(('panel', 'grp'))
Inputs may be any that keep to these rules, and one draw needn't show every extreme that they name: owner names every panel index once.
All inputs are finite; a program needn't handle non-finite values.
Results may differ from a plain program's by a relative error of at most 0.007.
Values may be sent and summed in bfloat16 or wider, within the bound.
No kernel may reach another device: no remote copies, remote signals or barrier semaphores. Data moves between devices by JAX's collectives and lax.ppermute only.
A program may use at most 128 MiB of HBM per device.

v0:
```python
import math

import jax
import jax.numpy as jnp
from jax import lax
from jax.sharding import PartitionSpec as P

NAUX = 16384
NV = 2048
NT = 2048


def spread(value, axis, root):
    mine = lax.axis_index(axis) == root
    return lax.psum(jnp.where(mine, value, jnp.zeros_like(value)), axis)


def on_device(b_blocks, w_store, owner, trials, eps_occ, eps_virt, slab_first):
    panels = lax.axis_size("panel")
    groups = lax.axis_size("grp")
    trial_rows = lax.all_gather(trials, "grp", axis=0, tiled=True)
    own_terms = jnp.dot(b_blocks, trial_rows, preferred_element_type=jnp.float32)
    projected_own = lax.psum(own_terms.astype(jnp.bfloat16), "panel")
    pieces = [spread(w_store, "panel", owner[member]) for member in range(panels)]
    w_rows = jnp.concatenate(pieces, axis=1)
    summed = lax.dot_general(
        lax.all_gather(b_blocks, "grp", axis=0, tiled=True),
        w_rows,
        (((0,), (1,)), ((), ())),
        preferred_element_type=jnp.float32,
    )
    kernel_local = (2.0 * b_blocks.astype(jnp.float32).T - summed).astype(jnp.bfloat16)
    kernel_rows = lax.all_to_all(kernel_local, "grp", split_axis=0, concat_axis=1, tiled=True)
    rows_here = kernel_rows.shape[0]
    first_row = (lax.axis_index("panel") * groups + lax.axis_index("grp")) * rows_here
    projected = lax.all_gather(projected_own, "grp", axis=0, tiled=True)
    coupling = jnp.dot(kernel_rows, projected, preferred_element_type=jnp.float32)
    occ_index = slab_first[0] + first_row // NV
    positions = jnp.arange(eps_occ.shape[0], dtype=jnp.int32)
    occupied = jnp.sum(jnp.where(positions == occ_index, eps_occ, 0.0))
    virtual = lax.dynamic_slice_in_dim(eps_virt, first_row % NV, rows_here, 0)
    diagonal = (virtual - occupied)[:, None]
    sigma = diagonal * trials.astype(jnp.float32) + coupling * (1.0 / math.sqrt(NAUX * NT))
    return (kernel_rows, sigma)


def solution(mesh):
    in_specs = (P("grp", "panel"), P("grp", "panel"), P(), P(("panel", "grp"), None), P(), P(), P())
    out_specs = (P(("panel", "grp"), None), P(("panel", "grp"), None))
    return jax.shard_map(
        on_device, mesh=mesh, in_specs=in_specs, out_specs=out_specs, check_vma=False
    )
```

profile of v0, /device:TPU:0, one launch (start us, length us, event | category | flops | bytes accessed | tf_op | source)
XLA Modules:
  0.0 575.7 jit_solution(13504006826066119364)
XLA Ops:
  8.0 0.0 all-reduce.3.cloned.1.call-start
  8.0 1.4 fusion.17
  12.0 97.2 %all_gather.10 = bf16[512,64]{1,0:T(8,128)(2,1)S(1)} all-gather(bf16[16,64]{1,0:T(8,128)(2,1)} %param.10), channel_id=1, replica_groups=mesh['panel'=4,'grp'=32] {'grp'}, dimensions={0}, use_global_device_ids=true | all-gather | bytes 67584 | tf_op jit(solution)/shard_map/all_gather | solution.py:21
  109.2 2.0 convolution_convert_fusion
  111.2 7.4 %broadcast_select_fusion.3 = (bf16[512,4096]{1,0:T(8,128)(2,1)}, bf16[512,4096]{1,0:T(8,128)(2,1)}, bf16[512,4096]{1,0:T(8,128)(2,1)}, bf16[512,4096]{1,0:T(8,128)(2,1)}) fusion(bf16[512,4096]{1,0:T(8,128)(2,1)} %param.8, pred[]{:T(512)S(6)} %eq.20, pred[]{:T(512)S(6)} %eq.21, pred[]{:T(512)S(6)} %eq.23, pred[]{:T(512)S(6)} %eq.22), kind=kLoop, calls=%fused_computation.11 | loop fusion | flops 8388608 | bytes 20971524 | tf_op jit(solution)/shard_map/jit(_where)/select_n | solution.py:15
  118.6 0.0 copy-start
  118.6 0.0 all-reduce.3.cloned.1.call-update
  118.6 0.0 all-gather.3.cloned.1.call-start
  118.7 0.5 all-gather.3.cloned.1.call-update
  119.2 0.0 all-gather.5.cloned.1.call-start
  119.2 0.4 copy-done
  119.6 0.2 copy.11
  119.9 368.7 %all-reduce.3.cloned.1.call-done = (bf16[512,4096]{1,0:T(8,128)(2,1)}, bf16[512,4096]{1,0:T(8,128)(2,1)}, bf16[512,4096]{1,0:T(8,128)(2,1)}, bf16[512,4096]{1,0:T(8,128)(2,1)}, bf16[512,64]{0,1:T(8,128)(2,1)}) async-done(((bf16[512,4096]{1,0:T(8,128)(2,1)}, bf16[512,4096]{1,0:T(8,128)(2,1)}, bf16[512,4096]{1,0:T(8,128)(2,1)}, bf16[512,4096]{1,0:T(8,128)(2,1)}, bf16[512,64]{0,1:T(8,128)(2,1)}), ...) | async-done | bytes 16842768 | tf_op jit(solution)/shard_map/psum | solution.py:15
  488.6 0.0 all-gather.5.cloned.1.call-update
  488.6 0.0 all-gather.3.cloned.1.call-done
  488.6 0.0 copy-start.3
  488.7 0.0 copy-start.2
  488.7 20.7 %fusion.11 = bf16[512,512]{0,1:T(8,128)(2,1)} fusion(bf16[16384,512]{1,0:T(8,128)(2,1)} %all-gather.3.cloned.1.call-done, bf16[512,4096]{1,0:T(8,128)(2,1)} %get-tuple-element.2, bf16[512,4096]{1,0:T(8,128)(2,1)} %get-tuple-element.3, bf16[512,4096]{1,0:T(8,128)(2,1)} %get-tuple-element.4, bf16[512,4096]{1,0:T(8,128)(2,1)} %get-tuple-element.5, ...), kind=kOutput, calls=%fused_computation.13 | convolution fusion | flops 8658092032 | bytes 34603008 | tf_op jit(solution)/shard_map/dot_general | solution.py:26
  509.3 9.4 %all-to-all-start = ((bf16[32,16,512]{2,1,0:T(8,128)(2,1)}), bf16[32,16,512]{2,1,0:T(8,128)(2,1)S(1)}, u32[]{:S(2)}, u32[]{:S(2)}) async-start(bf16[32,16,512]{2,1,0:T(8,128)(2,1)} %bitcast.5), calls=%async_computation | async-start | bytes 1048576 | tf_op jit(solution)/shard_map/all_to_all | solution.py:33
  519.4 0.0 copy-done.3
  519.4 0.6 fusion.15
  520.0 1.4 dynamic-slice_subtract_fusion
  521.4 11.9 %all-to-all-done = bf16[32,16,512]{2,1,0:T(8,128)(2,1)S(1)} async-done(((bf16[32,16,512]{2,1,0:T(8,128)(2,1)}), bf16[32,16,512]{2,1,0:T(8,128)(2,1)S(1)}, u32[]{:S(2)}, u32[]{:S(2)}) %all-to-all-start) | async-done | bytes 524320 | tf_op jit(solution)/shard_map/all_to_all | solution.py:33
  533.3 0.0 copy-start.1
  533.3 32.1 %all-gather.5.cloned.1.call-done = bf16[16384,64]{0,1:T(8,128)(2,1)} async-done(((bf16[512,64]{0,1:T(8,128)(2,1)}), bf16[16384,64]{0,1:T(8,128)(2,1)}) %all-gather.5.cloned.1.call-update) | async-done | bytes 2097168 | tf_op jit(solution)/shard_map/all_gather | solution.py:36
  565.4 0.0 copy-done.2
  565.4 2.8 fusion.14
  568.3 0.0 copy-done.1
  (1 shorter events, 0.0 us)
Async XLA Ops:
  8.0 480.6 %all-reduce.3.cloned.1.call-start = ((), (), s32[]{:S(2)}) async-start(), calls=%async_computation.3 | async-start | bytes 33685504 | tf_op jit(solution)/shard_map/psum | solution.py:15
  118.6 1.0 copy-start
  118.6 370.0 %all-gather.3.cloned.1.call-start = ((), (), s32[]{:S(2)}) async-start(), calls=%async_computation.1 | async-start | bytes 17301504 | tf_op jit(solution)/shard_map/all_gather | solution.py:27
  119.2 446.2 %all-gather.5.cloned.1.call-start = ((), (), s32[]{:S(2)}) async-start(), calls=%async_computation.2 | async-start | bytes 2162688 | tf_op jit(solution)/shard_map/all_gather | solution.py:36
  488.6 30.8 %copy-start.3 = (f32[128]{0:T(128)S(1)}, f32[128]{0:T(128)}, u32[]{:S(2)}) copy-start(f32[128]{0:T(128)} %param.11) | copy-start | bytes 1540
  488.7 76.8 %copy-start.2 = (bf16[16,64]{1,0:T(8,128)(2,1)S(1)}, bf16[16,64]{1,0:T(8,128)(2,1)}, u32[]{:S(2)}) copy-start(bf16[16,64]{1,0:T(8,128)(2,1)} %param.10) | copy-start | bytes 6148
  509.3 24.0 %all-to-all-start = ((bf16[32,16,512]{2,1,0:T(8,128)(2,1)}), bf16[32,16,512]{2,1,0:T(8,128)(2,1)S(1)}, u32[]{:S(2)}, u32[]{:S(2)}) async-start(bf16[32,16,512]{2,1,0:T(8,128)(2,1)} %bitcast.5), calls=%async_computation | async-start | bytes 1048576 | tf_op jit(solution)/shard_map/all_to_all | solution.py:33
  533.3 35.0 %copy-start.1 = (bf16[32,2,8,512]{3,2,0,1:T(8,128)(2,1)}, bf16[32,2,8,512]{3,2,0,1:T(8,128)(2,1)S(1)}, u32[]{:S(2)}) copy-start(bf16[32,2,8,512]{3,2,0,1:T(8,128)(2,1)S(1)} %copy.13) | copy-start | bytes 1572868
Sparse Core Ops, SparseCore 0:
  118.7 369.7 all-reduce.2
Sparse Core Ops, SparseCore 1:
  122.2 183.7 all-gather.2
  488.7 76.7 all-gather.4
where the time goes:
time: 576 us
  waiting for transfers between devices  413 us (72%)
  blocking collectives  97.2 us (17%)
  matrix products  25.5 us (4%)
  between operations  18.7 us (3%)
  starting transfers between devices  9.51 us (2%)
  other arithmetic  9.44 us (2%)
    psum x1, waiting for transfers between devices, spread(): return lax.psum(jnp.where(mine, value, jnp.zeros_like(value)), axis)  369 us
    all_gather x1, blocking collectives, on_device(): trial_rows = lax.all_gather(trials, 'grp', axis=0, tiled=True)  97.2 us
    all_gather x1, waiting for transfers between devices, on_device(): projected = lax.all_gather(projected_own, 'grp', axis=0, tiled=True)  32.1 us
    dot_general x1, matrix products, on_device(): lax.dot_general(lax.all_gather(b_blocks, 'grp', axis=0, tiled=True), w_ro...  20.7 us
    all_to_all x1, waiting for transfers between devices, on_device(): lax.all_to_all(kernel_local, 'grp', split_axis=0, concat_axis=1, tiled=True)  11.9 us
  transfers between devices with their start and end apart: 4, of which 3 were waited for; matrix products, arithmetic and copies ran while one was open for 4% of the time, Pallas kernels for 0%

commit v1 on v0

v1 whole, which is shorter than its diff:
```python
import math

import jax
import jax.numpy as jnp
from jax import lax
from jax.sharding import Mesh
from jax.sharding import PartitionSpec as P

NAUX = 16384
NV = 2048
NT = 2048
NVEC = 64

SIZES = {"xl": 2, "c": 2, "y": 4, "xh": 2, "z": 4}
AXES = tuple(SIZES)
GRP = ("y", "xh", "z")
PANEL = ("xl", "c")
PEERS = ("xl", "y", "xh", "z")


def move(value, axes, target):
    sizes = [SIZES[a] for a in axes]
    total = math.prod(sizes)
    pairs = []
    for source in range(total):
        rest, where = source, {}
        for axis, size in zip(reversed(axes), reversed(sizes)):
            rest, where[axis] = divmod(rest, size)
        there = target(where)
        if there is None:
            continue
        index = 0
        for axis, size in zip(axes, sizes):
            index = index * size + there[axis] % size
        pairs.append((source, index))
    return lax.ppermute(value, axes if len(axes) > 1 else axes[0], pairs)


def shift(value, axis, by):
    return move(value, (axis,), lambda w: {axis: w[axis] + by})


def along(value, by):
    return turn(value, by, 0)


def turn(value, by, x_core):
    def target(w):
        there = dict(w)
        if w["c"] == x_core:
            x = (2 * w["xh"] + w["xl"] + by) % 4
            there["xl"], there["xh"] = x % 2, x // 2
        else:
            there["z"] = w["z"] + by
        return there

    return move(value, ("xl", "c", "xh", "z"), target)


def keeps(w):
    return w["c"] == w["y"] % 2


def to_neighbour_plane(value, by):
    return move(
        value, ("c", "y"), lambda w: None if keeps(w) else {"c": 1 - w["c"], "y": w["y"] + by}
    )


def dot_tt(left, right):
    return lax.dot_general(
        left, right, (((1,), (1,)), ((), ())), preferred_element_type=jnp.float32
    )


def after(value, *others):
    return lax.optimization_barrier((value,) + others)[0]


def on_device(b_blocks, w_store, owner, trials, eps_occ, eps_virt, slab_first):
    xl, c, y = lax.axis_index("xl"), lax.axis_index("c"), lax.axis_index("y")
    xh, z = lax.axis_index("xh"), lax.axis_index("z")
    parity = lax.rem(y, 2)
    keeper = c == parity
    low = xl == 0
    first_core = c == 0

    bt = b_blocks.T.reshape(32, 2, 8, 512).transpose(1, 0, 2, 3).reshape(512, 512)
    from_below, from_above = shift(bt, "y", 1), shift(bt, "y", -1)
    from_across = shift(bt, "y", 2)

    def rows_of(place):
        plane = jnp.sum(jnp.where(owner == place, jnp.arange(4, dtype=jnp.int32), 0))
        off = lax.rem(y - plane + 4, 4)
        return jnp.where(
            off < 2,
            jnp.where(off == 0, bt, from_below),
            jnp.where(off == 2, from_across, from_above),
        )

    mine = rows_of(2 * xl + parity)
    theirs = rows_of(2 * (1 - xl) + parity)
    pair = jnp.stack([mine, theirs])

    p1, p2, p3 = along(pair, -1), along(pair, 2), along(pair, 1)

    w_late = after(w_store, pair)

    def column_blocks(rows):
        blocks = []
        for far in range(2):
            for step in range(4):
                group = jnp.where(far == 0, xh, 1 - xh) * 4 + lax.rem(z + step, 4)
                blocks.append(lax.dynamic_slice(w_late, (rows, group * 512), (256, 512)))
        return jnp.stack(blocks)

    w_lo, w_hi = column_blocks(0), column_blocks(256)
    below, above = to_neighbour_plane(w_lo, 1), to_neighbour_plane(w_hi, -1)
    swap_lo = shift(jnp.where(keeper, w_lo, below), "c", 1)
    swap_hi = shift(jnp.where(keeper, w_hi, above), "c", 1)
    w_all = jnp.stack(
        [
            jnp.where(keeper, w_lo, swap_lo),
            jnp.where(keeper, w_hi, swap_hi),
            jnp.where(keeper, swap_lo, below),
            jnp.where(keeper, swap_hi, above),
        ],
        axis=1,
    ).reshape(8, 1024, 512)

    def pick(core0, core1):
        return jnp.where(first_core, core0, core1)

    to_sides = jnp.stack([pick(mine, theirs), p1[1], pick(p2[0], p2[1]), p3[1]])
    to_across = jnp.stack([mine, pick(p1[1], p1[0]), p2[0], pick(p3[1], p3[0])])

    copies = jnp.broadcast_to(after(trials, p1, p2, p3), (32,) + trials.shape)
    trial_rows = lax.all_to_all(copies, GRP, split_axis=0, concat_axis=0).reshape(512, NVEC)
    terms = jnp.dot(b_blocks, trial_rows, preferred_element_type=jnp.float32)
    terms = terms + shift(terms, "c", 1)
    proj = (terms + shift(terms, "xl", 1)).astype(jnp.bfloat16)
    proj_rows = jnp.concatenate(
        [proj, shift(proj[:256], "y", 1), shift(proj[256:], "y", -1)], axis=0
    )

    def block(g, u):
        index = []
        for x_off, z_off in ((u, g), (g, u)):
            far = {0: 0, 2: 1, 1: 1 - low.astype(jnp.int32), 3: low.astype(jnp.int32)}[x_off]
            index.append(far * 4 + z_off)
        return lax.dynamic_index_in_dim(w_all, pick(*index), 0, keepdims=False)

    def finish(half):
        rows = slice(half * 256, half * 256 + 256)
        sides, across = to_sides[:, rows], to_across[:, rows]
        pieces = [across, turn(sides, -1, 1), turn(across, 2, 1), turn(sides, 1, 1)]
        sums = {}
        for g in (0, 1, 3, 2):
            for u in range(4):
                term = dot_tt(pieces[g][u], block(g, u))
                key = (g % 2, u % 2)
                sums[key] = sums[key] + term if key in sums else term
        same = sums[0, 0] + pick(sums[1, 0], sums[0, 1])
        opposite = sums[1, 1] + pick(sums[0, 1], sums[1, 0])
        twice = 2.0 * bt[rows].astype(jnp.float32)
        same = jnp.concatenate([twice - same[:, :512], -same[:, 512:]], axis=1)

        def message(part):
            rounded = part.astype(jnp.bfloat16)
            coupled = jnp.dot(rounded, proj_rows, preferred_element_type=jnp.float32)
            high = coupled.astype(jnp.bfloat16)
            rest = (coupled - high.astype(jnp.float32)).astype(jnp.bfloat16)
            return jnp.concatenate([rounded, high, rest], axis=1)

        m_same, m_opp = message(same), message(-opposite)
        out = jnp.stack([jnp.where(low, m_same, m_opp), jnp.where(low, m_opp, m_same)])
        got = lax.all_to_all(out.reshape(64, 8, 1152), PEERS, split_axis=0, concat_axis=0)
        got = got.astype(jnp.float32).reshape(2, 4, 8, 8, 1152).sum(axis=0)
        first = jnp.roll(got[..., 512:768], -1, axis=0)
        second = jnp.roll(got[..., 768:1024], 1, axis=0)
        kernel = got[..., :512] + jnp.concatenate([first, second], axis=-1)
        kernel = kernel.astype(jnp.bfloat16).transpose(2, 0, 1, 3).reshape(8, NAUX)
        return kernel, jnp.sum(got[..., 1024:1088] + got[..., 1088:], axis=(0, 1))

    halves = [finish(half) for half in range(2)]
    kernel_rows = jnp.concatenate([k for k, _ in halves], axis=0)
    coupling = jnp.concatenate([v for _, v in halves], axis=0)

    rows_here = 16
    first_row = ((xl * 2 + c) * 32 + y * 8 + xh * 4 + z) * rows_here
    occ_index = slab_first[0] + first_row // NV
    positions = jnp.arange(eps_occ.shape[0], dtype=jnp.int32)
    occupied = jnp.sum(jnp.where(positions == occ_index, eps_occ, 0.0))
    virtual = lax.dynamic_slice_in_dim(eps_virt, first_row % NV, rows_here, 0)
    diagonal = (virtual - occupied)[:, None]
    sigma = diagonal * trials.astype(jnp.float32) + coupling * (1.0 / math.sqrt(NAUX * NT))
    return (kernel_rows, sigma)


def solution(mesh):
    fine = Mesh(mesh.devices.reshape(tuple(SIZES.values())), AXES)
    in_specs = (P(GRP, PANEL), P(GRP, PANEL), P(), P(PANEL + GRP, None), P(), P(), P())
    out_specs = (P(PANEL + GRP, None), P(PANEL + GRP, None))
    return jax.shard_map(
        on_device, mesh=fine, in_specs=in_specs, out_specs=out_specs, check_vma=False
    )
```

time: 576 us -> 224 us (0.39)
  the two profiles are of different devices: /device:TPU:0 before, /device:TPU:1 now
where the time goes in v1:
time: 224 us; the launch traced here: 223 us
  waiting for transfers between devices  89.9 us (40%)
  starting transfers between devices  53.3 us (24%)
  other arithmetic  31.8 us (14%)
  matrix products  28.1 us (13%)
  local copies, waits for them, and re-layouts  16 us (7%)
  between operations  3.67 us (2%)
    ppermute x20, waiting for transfers between devices, move(): return lax.ppermute(value, axes if len(axes) > 1 else axes[0], pairs)  72.6 us
    ppermute x20, starting transfers between devices, move(): return lax.ppermute(value, axes if len(axes) > 1 else axes[0], pairs)  31.5 us
    dot_general x32, matrix products, dot_tt(): lax.dot_general(left, right, (((1,), (1,)), ((), ())), preferred_element_...  22.7 us
    all_to_all x2, waiting for transfers between devices, finish(): lax.all_to_all(out.reshape(64, 8, 1152), PEERS, split_axis=0, concat_axis=0)  17.3 us
    all_to_all x2, starting transfers between devices, finish(): lax.all_to_all(out.reshape(64, 8, 1152), PEERS, split_axis=0, concat_axis=0)  15 us
    unnamed x64, local copies, waits for them, and re-layouts  8.4 us
    all_to_all x1, starting transfers between devices, on_device(): lax.all_to_all(copies, GRP, split_axis=0, concat_axis=0).reshape(512, NVEC)  6.86 us
    another operation x3, other arithmetic, on_device(): jnp.stack([jnp.where(keeper, w_lo, swap_lo), jnp.where(keeper, w_hi, swap...  6.25 us
  transfers between devices with their start and end apart: 23, of which 10 were waited for; matrix products, arithmetic and copies ran while one was open for 25% of the time, Pallas kernels for 0%

profile of v1, /device:TPU:1, one launch (start us, length us, event | category | flops | bytes accessed | tf_op | source)
XLA Modules:
  0.0 222.8 jit_solution(6690051379782316441)
XLA Ops:
  0.6 1.3 copy.30
  2.0 2.2 collective-permute-start
  4.2 2.6 %collective-permute-start.1 = (bf16[512,512]{1,0:T(8,128)(2,1)S(1)}, bf16[512,512]{1,0:T(8,128)(2,1)S(1)}, u32[]{:S(2)}, u32[]{:S(2)}) collective-permute-start(bf16[512,512]{1,0:T(8,128)(2,1)S(1)} %bitcast.321), channel_id=1, source_target_pairs={{0,16},{8,24},{16,0},{24,8},{1,17},{9,25},{17,1},{25,9},{2,18},{10... | collective-permute-start | bytes 1572872 | tf_op jit(solution)/shard_map/ppermute | solution.py:36
  9.9 7.2 %collective-permute-done = bf16[512,512]{1,0:T(8,128)(2,1)S(1)} collective-permute-done((bf16[512,512]{1,0:T(8,128)(2,1)S(1)}, bf16[512,512]{1,0:T(8,128)(2,1)S(1)}, u32[]{:S(2)}, u32[]{:S(2)}) %collective-permute-start) | collective-permute-done | bytes 524320 | tf_op jit(solution)/shard_map/ppermute | solution.py:36
  17.1 12.2 %collective-permute-done.1 = bf16[512,512]{1,0:T(8,128)(2,1)S(1)} collective-permute-done((bf16[512,512]{1,0:T(8,128)(2,1)S(1)}, bf16[512,512]{1,0:T(8,128)(2,1)S(1)}, u32[]{:S(2)}, u32[]{:S(2)}) %collective-permute-start.1) | collective-permute-done | bytes 524320 | tf_op jit(solution)/shard_map/ppermute | solution.py:36
  37.5 4.3 %collective-permute-start.3 = (bf16[8,256,512]{2,1,0:T(8,128)(2,1)S(1)}, bf16[8,256,512]{2,1,0:T(8,128)(2,1)}, u32[]{:S(2)}, u32[]{:S(2)}) collective-permute-start(bf16[8,256,512]{2,1,0:T(8,128)(2,1)S(1)} %get-tuple-element.13), channel_id=1, source_target_pairs={{8,48},{24,32},{32,8},{48,24},{9,49},{25,33},{33,9},{49,25},{10,50... | collective-permute-start | bytes 6291464 | tf_op jit(solution)/shard_map/ppermute | solution.py:36
  41.7 3.8 %collective-permute-start.8 = (bf16[2,512,512]{2,1,0:T(8,128)(2,1)}, bf16[2,512,512]{2,1,0:T(8,128)(2,1)}, u32[]{:S(2)}, u32[]{:S(2)}) collective-permute-start(bf16[2,512,512]{2,1,0:T(8,128)(2,1)} %pad_maximum_fusion.5), channel_id=1, source_target_pairs={{0,68},{1,69},{2,70},{3,71},{4,64},{5,65},{6,66},{7,67},{32,35},{3... | collective-permute-start | bytes 3145736 | tf_op jit(solution)/shard_map/ppermute | solution.py:36
  46.3 2.8 %collective-permute-start.5 = (bf16[8,256,512]{2,1,0:T(8,128)(2,1)}, bf16[8,256,512]{2,1,0:T(8,128)(2,1)}, u32[]{:S(2)}, u32[]{:S(2)}) collective-permute-start(bf16[8,256,512]{2,1,0:T(8,128)(2,1)} %get-tuple-element.14), channel_id=1, source_target_pairs={{8,32},{24,48},{32,24},{48,8},{9,33},{25,49},{33,25},{49,9},{10,34... | collective-permute-start | bytes 6291464 | tf_op jit(solution)/shard_map/ppermute | solution.py:36
  49.2 19.7 %collective-permute-done.8 = bf16[2,512,512]{2,1,0:T(8,128)(2,1)} collective-permute-done((bf16[2,512,512]{2,1,0:T(8,128)(2,1)}, bf16[2,512,512]{2,1,0:T(8,128)(2,1)}, u32[]{:S(2)}, u32[]{:S(2)}) %collective-permute-start.8) | collective-permute-done | bytes 1048608 | tf_op jit(solution)/shard_map/ppermute | solution.py:36
  68.9 3.1 %collective-permute-done.9 = bf16[2,512,512]{2,1,0:T(8,128)(2,1)} collective-permute-done((bf16[2,512,512]{2,1,0:T(8,128)(2,1)}, bf16[2,512,512]{2,1,0:T(8,128)(2,1)}, u32[]{:S(2)}, u32[]{:S(2)}) %collective-permute-start.9) | collective-permute-done | bytes 1048608 | tf_op jit(solution)/shard_map/ppermute | solution.py:36
  72.8 6.9 %all-to-all-start = ((bf16[32,2,512]{2,1,0:T(2,128)(2,1)}), bf16[32,2,512]{2,1,0:T(2,128)(2,1)S(1)}, u32[]{:S(2)}, u32[]{:S(2)}) async-start(bf16[32,2,512]{2,1,0:T(2,128)(2,1)} %reshape.429), calls=%async_computation | async-start | bytes 131072 | tf_op jit(solution)/shard_map/all_to_all | solution.py:138
  79.6 1.3 slice_select_fusion.2
  80.9 1.3 fusion.157
  82.2 3.1 %broadcast_select_fusion.1 = bf16[8,256,512]{2,1,0:T(8,128)(2,1)} fusion(bf16[8,256,512]{2,1,0:T(8,128)(2,1)S(1)} %get-tuple-element.13, bf16[8,256,512]{2,1,0:T(8,128)(2,1)} %collective-permute-done.3, pred[]{:T(512)S(6)} %eq.46), kind=kLoop, calls=%fused_computation.10 | loop fusion | flops 1048576 | bytes 6291457 | tf_op jit(solution)/shard_map/jit(_where)/select_n | solution.py:119
  85.3 1.3 slice_select_fusion.1
  86.6 3.5 %broadcast_select_fusion = bf16[8,256,512]{2,1,0:T(8,128)(2,1)} fusion(bf16[8,256,512]{2,1,0:T(8,128)(2,1)} %get-tuple-element.14, bf16[8,256,512]{2,1,0:T(8,128)(2,1)} %collective-permute-done.5, pred[]{:T(512)S(6)} %eq.46), kind=kLoop, calls=%fused_computation.9 | loop fusion | flops 1048576 | bytes 6291457 | tf_op jit(solution)/shard_map/jit(_where)/select_n | solution.py:120
  90.6 2.3 %pad_maximum_fusion.1 = (bf16[4,512,512]{2,1,0:T(8,128)(2,1)}, bf16[4,512,512]{2,1,0:T(8,128)(2,1)}) fusion(bf16[1,512,512]{2,1,0:T(8,128)(2,1)S(1)} %get-tuple-element.57, bf16[1,512,512]{2,1,0:T(8,128)(2,1)S(1)} %get-tuple-element.55, bf16[1,512,512]{2,1,0:T(8,128)(2,1)S(1)} %get-tuple-element.53, bf16[1,512,512]{2,1,0:T(8,128)(2,1)S(1)} %bitcast.313, ...), kind=kLoop, calls=%fused_computation.3 | loop fusion | flops 6291456 | bytes 8388608 | tf_op jit(solution)/shard_map/stack | solution.py:135
  93.0 1.3 convolution_bitcast_fusion
  94.4 1.9 fusion.152
  96.7 2.4 %collective-permute-start.11 = (bf16[4,256,512]{2,1,0:T(8,128)(2,1)S(1)}, bf16[4,256,512]{2,1,0:T(8,128)(2,1)S(1)}, u32[]{:S(2)}, u32[]{:S(2)}) collective-permute-start(bf16[4,256,512]{2,1,0:T(8,128)(2,1)S(1)} %get-tuple-element.31), channel_id=1, source_target_pairs={{0,3},{1,0},{2,1},{3,2},{4,7},{5,4},{6,5},{7,6},{32,100},{33,101},... | collective-permute-start | bytes 3145736 | tf_op jit(solution)/shard_map/ppermute | solution.py:36
  99.5 14.7 %collective-permute-done.14 = f32[512,64]{0,1:T(8,128)S(1)} collective-permute-done((f32[512,64]{0,1:T(8,128)S(1)}, f32[512,64]{0,1:T(8,128)S(1)}, u32[]{:S(2)}, u32[]{:S(2)}) %collective-permute-start.14) | collective-permute-done | bytes 131104 | tf_op jit(solution)/shard_map/ppermute | solution.py:36
  114.1 1.5 collective-permute-start.18
  115.8 2.6 %select_bitcast_fusion.3 = (bf16[8,1,256,512]{3,2,1,0:T(8,128)(2,1)S(1)}, bf16[8,1,256,512]{3,2,1,0:T(8,128)(2,1)S(1)}) fusion(bf16[8,256,512]{2,1,0:T(8,128)(2,1)S(1)} %get-tuple-element.13, bf16[8,256,512]{2,1,0:T(8,128)(2,1)} %collective-permute-done.4, pred[]{:T(512)S(6)} %eq.46, bf16[8,256,512]{2,1,0:T(8,128)(2,1)} %collective-permute-done.3), kind=kLoop, calls=%fused_computation.8 | loop fusion | flops 2097152 | bytes 10485761 | tf_op jit(solution)/shard_map/stack | solution.py:121
  118.4 2.7 %collective-permute-start.10 = (bf16[4,256,512]{2,1,0:T(8,128)(2,1)S(1)}, bf16[4,256,512]{2,1,0:T(8,128)(2,1)S(1)}, u32[]{:S(2)}, u32[]{:S(2)}) collective-permute-start(bf16[4,256,512]{2,1,0:T(8,128)(2,1)S(1)} %get-tuple-element.29), channel_id=1, source_target_pairs={{0,2},{1,3},{2,0},{3,1},{4,6},{5,7},{6,4},{7,5},{32,36},{33,37},{3... | collective-permute-start | bytes 3145736 | tf_op jit(solution)/shard_map/ppermute | solution.py:36
  121.1 2.6 %select_bitcast_fusion.2 = (bf16[8,1,256,512]{3,2,1,0:T(8,128)(2,1)S(1)}, bf16[8,1,256,512]{3,2,1,0:T(8,128)(2,1)S(1)}) fusion(bf16[8,256,512]{2,1,0:T(8,128)(2,1)} %get-tuple-element.14, bf16[8,256,512]{2,1,0:T(8,128)(2,1)} %collective-permute-done.6, pred[]{:T(512)S(6)} %eq.46, bf16[8,256,512]{2,1,0:T(8,128)(2,1)} %collective-permute-done.5), kind=kLoop, calls=%fused_computation.7 | loop fusion | flops 2097152 | bytes 10485761 | tf_op jit(solution)/shard_map/stack | solution.py:121
  123.7 1.1 pad_maximum_fusion
  127.1 3.8 %collective-permute-done.19 = bf16[4,256,512]{2,1,0:T(8,128)(2,1)S(1)} collective-permute-done((bf16[4,256,512]{2,1,0:T(8,128)(2,1)S(1)}, bf16[4,256,512]{2,1,0:T(8,128)(2,1)S(1)}, u32[]{:S(2)}, u32[]{:S(2)}) %collective-permute-start.19) | collective-permute-done | bytes 1048608 | tf_op jit(solution)/shard_map/ppermute | solution.py:36
  130.9 2.3 %collective-permute-start.15 = (bf16[256,64]{0,1:T(8,128)(2,1)S(1)}, bf16[256,64]{0,1:T(8,128)(2,1)S(1)}, u32[]{:S(2)}, u32[]{:S(2)}) collective-permute-start(bf16[256,64]{0,1:T(8,128)(2,1)S(1)} %get-tuple-element.69), channel_id=1, source_target_pairs={{0,8},{8,16},{16,24},{24,0},{1,9},{9,17},{17,25},{25,1},{2,10},{10... | collective-permute-start | bytes 98312 | tf_op jit(solution)/shard_map/ppermute | solution.py:36
  134.2 1.4 fusion.62
  135.6 1.4 fusion.64
  137.0 5.1 %collective-permute-done.10 = bf16[4,256,512]{2,1,0:T(8,128)(2,1)S(1)} collective-permute-done((bf16[4,256,512]{2,1,0:T(8,128)(2,1)S(1)}, bf16[4,256,512]{2,1,0:T(8,128)(2,1)S(1)}, u32[]{:S(2)}, u32[]{:S(2)}) %collective-permute-start.10) | collective-permute-done | bytes 1048608 | tf_op jit(solution)/shard_map/ppermute | solution.py:36
  142.1 3.5 %collective-permute-start.16 = (bf16[256,64]{0,1:T(8,128)(2,1)S(1)}, bf16[256,64]{0,1:T(8,128)(2,1)S(1)}, u32[]{:S(2)}, u32[]{:S(2)}) collective-permute-start(bf16[256,64]{0,1:T(8,128)(2,1)S(1)} %get-tuple-element.70), channel_id=1, source_target_pairs={{0,24},{8,0},{16,8},{24,16},{1,25},{9,1},{17,9},{25,17},{2,26},{10... | collective-permute-start | bytes 98312 | tf_op jit(solution)/shard_map/ppermute | solution.py:36
  146.4 6.7 %collective-permute-done.17 = bf16[4,256,512]{2,1,0:T(8,128)(2,1)S(1)} collective-permute-done((bf16[4,256,512]{2,1,0:T(8,128)(2,1)S(1)}, bf16[4,256,512]{2,1,0:T(8,128)(2,1)S(1)}, u32[]{:S(2)}, u32[]{:S(2)}) %collective-permute-start.17) | collective-permute-done | bytes 1048608 | tf_op jit(solution)/shard_map/ppermute | solution.py:36
  167.1 2.0 fusion.110
  169.0 1.2 concatenate.152
  170.4 1.1 pad_maximum_fusion.3
  171.5 8.5 %all-to-all-start.1 = ((bf16[64,8,1152]{2,1,0:T(8,128)(2,1)}), bf16[64,8,1152]{2,1,0:T(8,128)(2,1)S(1)}, u32[]{:S(2)}, u32[]{:S(2)}) async-start(bf16[64,8,1152]{2,1,0:T(8,128)(2,1)} %bitcast.319), calls=%async_computation.1 | async-start | bytes 2359296 | tf_op jit(solution)/shard_map/all_to_all | solution.py:177
  180.0 1.9 fusion.28
  181.8 1.7 fusion.24
  183.5 1.7 fusion.20
  185.3 1.9 fusion.19
  188.0 1.2 concatenate.168
  191.4 1.2 pad_maximum_fusion.4
  192.6 3.2 %all-to-all-done.1 = bf16[64,8,1152]{2,1,0:T(8,128)(2,1)S(1)} async-done(((bf16[64,8,1152]{2,1,0:T(8,128)(2,1)}), bf16[64,8,1152]{2,1,0:T(8,128)(2,1)S(1)}, u32[]{:S(2)}, u32[]{:S(2)}) %all-to-all-start.1) | async-done | bytes 1179680 | tf_op jit(solution)/shard_map/all_to_all | solution.py:177
  195.8 6.5 %all-to-all-start.2 = ((bf16[64,8,1152]{2,1,0:T(8,128)(2,1)}), bf16[64,8,1152]{2,1,0:T(8,128)(2,1)}, u32[]{:S(2)}, u32[]{:S(2)}) async-start(bf16[64,8,1152]{2,1,0:T(8,128)(2,1)} %bitcast.101), calls=%async_computation.2 | async-start | bytes 2359296 | tf_op jit(solution)/shard_map/all_to_all | solution.py:177
  203.5 1.4 dynamic-slice_subtract_fusion
  205.3 14.1 %all-to-all-done.2 = bf16[64,8,1152]{2,1,0:T(8,128)(2,1)} async-done(((bf16[64,8,1152]{2,1,0:T(8,128)(2,1)}), bf16[64,8,1152]{2,1,0:T(8,128)(2,1)}, u32[]{:S(2)}, u32[]{:S(2)}) %all-to-all-start.2) | async-done | bytes 1179680 | tf_op jit(solution)/shard_map/all_to_all | solution.py:177
  219.4 1.6 convert_reduce_fusion
  (145 shorter events, 36.3 us)
Async XLA Ops:
  0.6 7.2 %copy-start.19 = (s32[4]{0:T(128)S(1)}, s32[4]{0:T(128)}, u32[]{:S(2)}) copy-start(s32[4]{0:T(128)} %param.9) | copy-start | bytes 52
  1.9 27.4 %copy-start.4 = (bf16[512,512]{0,1:T(8,128)(2,1)}, bf16[512,512]{0,1:T(8,128)(2,1)S(1)}, u32[]{:S(2)}) copy-start(bf16[512,512]{0,1:T(8,128)(2,1)S(1)} %copy.30) | copy-start | bytes 1572868
  2.0 15.1 %collective-permute-start = (bf16[512,512]{1,0:T(8,128)(2,1)S(1)}, bf16[512,512]{1,0:T(8,128)(2,1)S(1)}, u32[]{:S(2)}, u32[]{:S(2)}) collective-permute-start(bf16[512,512]{1,0:T(8,128)(2,1)S(1)} %bitcast.320), channel_id=1, source_target_pairs={{0,8},{8,16},{16,24},{24,0},{1,9},{9,17},{17,25},{25,1},{2,10},{10... | collective-permute-start | bytes 1572872 | tf_op jit(solution)/shard_map/ppermute | solution.py:36
  4.2 25.2 %collective-permute-start.1 = (bf16[512,512]{1,0:T(8,128)(2,1)S(1)}, bf16[512,512]{1,0:T(8,128)(2,1)S(1)}, u32[]{:S(2)}, u32[]{:S(2)}) collective-permute-start(bf16[512,512]{1,0:T(8,128)(2,1)S(1)} %bitcast.321), channel_id=1, source_target_pairs={{0,16},{8,24},{16,0},{24,8},{1,17},{9,25},{17,1},{25,9},{2,18},{10... | collective-permute-start | bytes 1572872 | tf_op jit(solution)/shard_map/ppermute | solution.py:36
  6.8 22.6 %collective-permute-start.2 = (bf16[512,512]{1,0:T(8,128)(2,1)S(1)}, bf16[512,512]{1,0:T(8,128)(2,1)S(1)}, u32[]{:S(2)}, u32[]{:S(2)}) collective-permute-start(bf16[512,512]{1,0:T(8,128)(2,1)S(1)} %bitcast.322), channel_id=1, source_target_pairs={{0,24},{8,0},{16,8},{24,16},{1,25},{9,1},{17,9},{25,17},{2,26},{10... | collective-permute-start | bytes 1572872 | tf_op jit(solution)/shard_map/ppermute | solution.py:36
  9.9 21.6 %copy-start.6 = (bf16[512,4096]{1,0:T(8,128)(2,1)S(1)}, bf16[512,4096]{1,0:T(8,128)(2,1)}, u32[]{:S(2)}) copy-start(bf16[512,4096]{1,0:T(8,128)(2,1)} %param.8) | copy-start | bytes 12582916
  34.4 37.5 %copy-start.18 = (bf16[16,64]{1,0:T(8,128)(2,1)S(1)}, bf16[16,64]{1,0:T(8,128)(2,1)}, u32[]{:S(2)}) copy-start(bf16[16,64]{1,0:T(8,128)(2,1)} %param.10) | copy-start | bytes 6148
  37.5 44.7 %collective-permute-start.3 = (bf16[8,256,512]{2,1,0:T(8,128)(2,1)S(1)}, bf16[8,256,512]{2,1,0:T(8,128)(2,1)}, u32[]{:S(2)}, u32[]{:S(2)}) collective-permute-start(bf16[8,256,512]{2,1,0:T(8,128)(2,1)S(1)} %get-tuple-element.13), channel_id=1, source_target_pairs={{8,48},{24,32},{32,8},{48,24},{9,49},{25,33},{33,9},{49,25},{10,50... | collective-permute-start | bytes 6291464 | tf_op jit(solution)/shard_map/ppermute | solution.py:36
  41.7 27.1 %collective-permute-start.8 = (bf16[2,512,512]{2,1,0:T(8,128)(2,1)}, bf16[2,512,512]{2,1,0:T(8,128)(2,1)}, u32[]{:S(2)}, u32[]{:S(2)}) collective-permute-start(bf16[2,512,512]{2,1,0:T(8,128)(2,1)} %pad_maximum_fusion.5), channel_id=1, source_target_pairs={{0,68},{1,69},{2,70},{3,71},{4,64},{5,65},{6,66},{7,67},{32,35},{3... | collective-permute-start | bytes 3145736 | tf_op jit(solution)/shard_map/ppermute | solution.py:36
  45.6 23.3 %collective-permute-start.7 = (bf16[2,512,512]{2,1,0:T(8,128)(2,1)}, bf16[2,512,512]{2,1,0:T(8,128)(2,1)}, u32[]{:S(2)}, u32[]{:S(2)}) collective-permute-start(bf16[2,512,512]{2,1,0:T(8,128)(2,1)} %pad_maximum_fusion.5), channel_id=1, source_target_pairs={{0,4},{1,5},{2,6},{3,7},{4,0},{5,1},{6,2},{7,3},{32,34},{33,35},{3... | collective-permute-start | bytes 3145736 | tf_op jit(solution)/shard_map/ppermute | solution.py:36
  45.6 26.4 %collective-permute-start.9 = (bf16[2,512,512]{2,1,0:T(8,128)(2,1)}, bf16[2,512,512]{2,1,0:T(8,128)(2,1)}, u32[]{:S(2)}, u32[]{:S(2)}) collective-permute-start(bf16[2,512,512]{2,1,0:T(8,128)(2,1)} %pad_maximum_fusion.5), channel_id=1, source_target_pairs={{0,64},{1,65},{2,66},{3,67},{4,68},{5,69},{6,70},{7,71},{32,33},{3... | collective-permute-start | bytes 3145736 | tf_op jit(solution)/shard_map/ppermute | solution.py:36
  46.3 40.4 %collective-permute-start.5 = (bf16[8,256,512]{2,1,0:T(8,128)(2,1)}, bf16[8,256,512]{2,1,0:T(8,128)(2,1)}, u32[]{:S(2)}, u32[]{:S(2)}) collective-permute-start(bf16[8,256,512]{2,1,0:T(8,128)(2,1)} %get-tuple-element.14), channel_id=1, source_target_pairs={{8,32},{24,48},{32,24},{48,8},{9,33},{25,49},{33,25},{49,9},{10,34... | collective-permute-start | bytes 6291464 | tf_op jit(solution)/shard_map/ppermute | solution.py:36
  72.8 20.1 %all-to-all-start = ((bf16[32,2,512]{2,1,0:T(2,128)(2,1)}), bf16[32,2,512]{2,1,0:T(2,128)(2,1)S(1)}, u32[]{:S(2)}, u32[]{:S(2)}) async-start(bf16[32,2,512]{2,1,0:T(2,128)(2,1)} %reshape.429), calls=%async_computation | async-start | bytes 131072 | tf_op jit(solution)/shard_map/all_to_all | solution.py:138
  85.3 30.4 %collective-permute-start.4 = (bf16[8,256,512]{2,1,0:T(8,128)(2,1)}, bf16[8,256,512]{2,1,0:T(8,128)(2,1)}, u32[]{:S(2)}, u32[]{:S(2)}) collective-permute-start(bf16[8,256,512]{2,1,0:T(8,128)(2,1)} %broadcast_select_fusion.1), channel_id=1, source_target_pairs={{0,32},{32,0},{1,33},{33,1},{2,34},{34,2},{3,35},{35,3},{4,36},{36... | collective-permute-start | bytes 6291464 | tf_op jit(solution)/shard_map/ppermute | solution.py:36
  86.6 4.0 %copy-start.2 = (bf16[1,512,512]{2,1,0:T(8,128)(2,1)}, bf16[1,512,512]{2,1,0:T(8,128)(2,1)S(1)}, u32[]{:S(2)}) copy-start(bf16[1,512,512]{2,1,0:T(8,128)(2,1)S(1)} %get-tuple-element.57) | copy-start | bytes 1572868
  86.6 4.0 %copy-start.7 = (bf16[1,512,512]{2,1,0:T(8,128)(2,1)S(1)}, bf16[1,512,512]{2,1,0:T(8,128)(2,1)}, u32[]{:S(2)}) copy-start(bf16[1,512,512]{2,1,0:T(8,128)(2,1)} %get-tuple-element.8) | copy-start | bytes 1572868
  90.1 28.3 %collective-permute-start.6 = (bf16[8,256,512]{2,1,0:T(8,128)(2,1)}, bf16[8,256,512]{2,1,0:T(8,128)(2,1)}, u32[]{:S(2)}, u32[]{:S(2)}) collective-permute-start(bf16[8,256,512]{2,1,0:T(8,128)(2,1)} %broadcast_select_fusion), channel_id=1, source_target_pairs={{0,32},{32,0},{1,33},{33,1},{2,34},{34,2},{3,35},{35,3},{4,36},{36... | collective-permute-start | bytes 6291464 | tf_op jit(solution)/shard_map/ppermute | solution.py:36
  94.3 4.8 %collective-permute-start.13 = (f32[512,64]{0,1:T(8,128)S(1)}, f32[512,64]{0,1:T(8,128)S(1)}, u32[]{:S(2)}, u32[]{:S(2)}) collective-permute-start(f32[512,64]{0,1:T(8,128)S(1)} %convolution_bitcast_fusion), channel_id=1, source_target_pairs={{0,32},{32,0},{1,33},{33,1},{2,34},{34,2},{3,35},{35,3},{4,36},{36... | collective-permute-start | bytes 393224 | tf_op jit(solution)/shard_map/ppermute | solution.py:36
  94.4 4.8 %copy-start.1 = (bf16[4,512,512]{2,1,0:T(8,128)(2,1)S(1)}, bf16[4,512,512]{2,1,0:T(8,128)(2,1)}, u32[]{:S(2)}) copy-start(bf16[4,512,512]{2,1,0:T(8,128)(2,1)} %get-tuple-element.71) | copy-start | bytes 6291460
  96.3 29.4 %collective-permute-start.12 = (bf16[4,256,512]{2,1,0:T(8,128)(2,1)S(1)}, bf16[4,256,512]{2,1,0:T(8,128)(2,1)S(1)}, u32[]{:S(2)}, u32[]{:S(2)}) collective-permute-start(bf16[4,256,512]{2,1,0:T(8,128)(2,1)S(1)} %get-tuple-element.31), channel_id=1, source_target_pairs={{0,1},{1,2},{2,3},{3,0},{4,5},{5,6},{6,7},{7,4},{32,96},{33,97},{3... | collective-permute-start | bytes 3145736 | tf_op jit(solution)/shard_map/ppermute | solution.py:36
  96.7 58.3 %collective-permute-start.11 = (bf16[4,256,512]{2,1,0:T(8,128)(2,1)S(1)}, bf16[4,256,512]{2,1,0:T(8,128)(2,1)S(1)}, u32[]{:S(2)}, u32[]{:S(2)}) collective-permute-start(bf16[4,256,512]{2,1,0:T(8,128)(2,1)S(1)} %get-tuple-element.31), channel_id=1, source_target_pairs={{0,3},{1,0},{2,1},{3,2},{4,7},{5,4},{6,5},{7,6},{32,100},{33,101},... | collective-permute-start | bytes 3145736 | tf_op jit(solution)/shard_map/ppermute | solution.py:36
  99.1 15.0 %collective-permute-start.14 = (f32[512,64]{0,1:T(8,128)S(1)}, f32[512,64]{0,1:T(8,128)S(1)}, u32[]{:S(2)}, u32[]{:S(2)}) collective-permute-start(f32[512,64]{0,1:T(8,128)S(1)} %add.357), channel_id=1, source_target_pairs={{0,64},{64,0},{1,65},{65,1},{2,66},{66,2},{3,67},{67,3},{4,68},{68... | collective-permute-start | bytes 393224 | tf_op jit(solution)/shard_map/ppermute | solution.py:36
  114.1 42.8 %collective-permute-start.18 = (bf16[4,256,512]{2,1,0:T(8,128)(2,1)S(1)}, bf16[4,256,512]{2,1,0:T(8,128)(2,1)S(1)}, u32[]{:S(2)}, u32[]{:S(2)}) collective-permute-start(bf16[4,256,512]{2,1,0:T(8,128)(2,1)S(1)} %get-tuple-element.32), channel_id=1, source_target_pairs={{0,3},{1,0},{2,1},{3,2},{4,7},{5,4},{6,5},{7,6},{32,100},{33,101},... | collective-permute-start | bytes 3145736 | tf_op jit(solution)/shard_map/ppermute | solution.py:36
  115.7 49.5 %copy-start.15 = (bf16[512,64]{0,1:T(8,128)(2,1)}, bf16[512,64]{0,1:T(8,128)(2,1)S(1)}, u32[]{:S(2)}) copy-start(bf16[512,64]{0,1:T(8,128)(2,1)S(1)} %add_convert_fusion) | copy-start | bytes 196612
  115.7 15.2 %collective-permute-start.19 = (bf16[4,256,512]{2,1,0:T(8,128)(2,1)S(1)}, bf16[4,256,512]{2,1,0:T(8,128)(2,1)S(1)}, u32[]{:S(2)}, u32[]{:S(2)}) collective-permute-start(bf16[4,256,512]{2,1,0:T(8,128)(2,1)S(1)} %get-tuple-element.32), channel_id=1, source_target_pairs={{0,1},{1,2},{2,3},{3,0},{4,5},{5,6},{6,7},{7,4},{32,96},{33,97},{3... | collective-permute-start | bytes 3145736 | tf_op jit(solution)/shard_map/ppermute | solution.py:36
  118.4 23.8 %collective-permute-start.10 = (bf16[4,256,512]{2,1,0:T(8,128)(2,1)S(1)}, bf16[4,256,512]{2,1,0:T(8,128)(2,1)S(1)}, u32[]{:S(2)}, u32[]{:S(2)}) collective-permute-start(bf16[4,256,512]{2,1,0:T(8,128)(2,1)S(1)} %get-tuple-element.29), channel_id=1, source_target_pairs={{0,2},{1,3},{2,0},{3,1},{4,6},{5,7},{6,4},{7,5},{32,36},{33,37},{3... | collective-permute-start | bytes 3145736 | tf_op jit(solution)/shard_map/ppermute | solution.py:36
  123.6 1.1 copy-start.3
  124.8 38.9 %copy-start = (bf16[8,4,256,512]{3,2,1,0:T(8,128)(2,1)}, bf16[8,4,256,512]{3,2,1,0:T(8,128)(2,1)S(1)}, u32[]{:S(2)}) copy-start(bf16[8,4,256,512]{3,2,1,0:T(8,128)(2,1)S(1)} %pad_maximum_fusion) | copy-start | bytes 25165828
  125.8 27.3 %collective-permute-start.17 = (bf16[4,256,512]{2,1,0:T(8,128)(2,1)S(1)}, bf16[4,256,512]{2,1,0:T(8,128)(2,1)S(1)}, u32[]{:S(2)}, u32[]{:S(2)}) collective-permute-start(bf16[4,256,512]{2,1,0:T(8,128)(2,1)S(1)} %get-tuple-element.30), channel_id=1, source_target_pairs={{0,2},{1,3},{2,0},{3,1},{4,6},{5,7},{6,4},{7,5},{32,36},{33,37},{3... | collective-permute-start | bytes 3145736 | tf_op jit(solution)/shard_map/ppermute | solution.py:36
  130.9 3.2 %copy-start.12 = (bf16[4,256,512]{2,1,0:T(8,128)(2,1)}, bf16[4,256,512]{2,1,0:T(8,128)(2,1)S(1)}, u32[]{:S(2)}) copy-start(bf16[4,256,512]{2,1,0:T(8,128)(2,1)S(1)} %collective-permute-done.19) | copy-start | bytes 3145732
  130.9 34.2 %collective-permute-start.15 = (bf16[256,64]{0,1:T(8,128)(2,1)S(1)}, bf16[256,64]{0,1:T(8,128)(2,1)S(1)}, u32[]{:S(2)}, u32[]{:S(2)}) collective-permute-start(bf16[256,64]{0,1:T(8,128)(2,1)S(1)} %get-tuple-element.69), channel_id=1, source_target_pairs={{0,8},{8,16},{16,24},{24,0},{1,9},{9,17},{17,25},{25,1},{2,10},{10... | collective-permute-start | bytes 98312 | tf_op jit(solution)/shard_map/ppermute | solution.py:36
  142.1 23.0 %collective-permute-start.16 = (bf16[256,64]{0,1:T(8,128)(2,1)S(1)}, bf16[256,64]{0,1:T(8,128)(2,1)S(1)}, u32[]{:S(2)}, u32[]{:S(2)}) collective-permute-start(bf16[256,64]{0,1:T(8,128)(2,1)S(1)} %get-tuple-element.70), channel_id=1, source_target_pairs={{0,24},{8,0},{16,8},{24,16},{1,25},{9,1},{17,9},{25,17},{2,26},{10... | collective-permute-start | bytes 98312 | tf_op jit(solution)/shard_map/ppermute | solution.py:36
  156.9 2.0 copy-start.14
  160.1 1.0 copy-start.5
  162.2 2.0 copy-start.10
  162.2 2.0 copy-start.11
  165.1 0.9 copy-start.20
  171.5 24.3 %all-to-all-start.1 = ((bf16[64,8,1152]{2,1,0:T(8,128)(2,1)}), bf16[64,8,1152]{2,1,0:T(8,128)(2,1)S(1)}, u32[]{:S(2)}, u32[]{:S(2)}) async-start(bf16[64,8,1152]{2,1,0:T(8,128)(2,1)} %bitcast.319), calls=%async_computation.1 | async-start | bytes 2359296 | tf_op jit(solution)/shard_map/all_to_all | solution.py:177
  180.0 1.9 copy-start.13
  185.2 2.0 copy-start.16
  185.3 2.0 copy-start.21
  185.3 2.0 copy-start.24
  187.3 2.0 copy-start.9
  187.3 2.0 copy-start.17
  187.3 2.0 copy-start.22
  187.3 2.0 copy-start.25
  191.4 11.6 %copy-start.26 = (f32[128]{0:T(128)S(1)}, f32[128]{0:T(128)}, u32[]{:S(2)}) copy-start(f32[128]{0:T(128)} %param.11) | copy-start | bytes 1540
  195.8 23.7 %all-to-all-start.2 = ((bf16[64,8,1152]{2,1,0:T(8,128)(2,1)}), bf16[64,8,1152]{2,1,0:T(8,128)(2,1)}, u32[]{:S(2)}, u32[]{:S(2)}) async-start(bf16[64,8,1152]{2,1,0:T(8,128)(2,1)} %bitcast.101), calls=%async_computation.2 | async-start | bytes 2359296 | tf_op jit(solution)/shard_map/all_to_all | solution.py:177
  (2 other events, 1.7 us)

commit v2 on v1

v2 whole, which is shorter than its diff:
```python
import math

import jax
import jax.numpy as jnp
from jax import lax
from jax.experimental import pallas as pl
from jax.experimental.pallas import tpu as pltpu
from jax.sharding import Mesh
from jax.sharding import PartitionSpec as P

NAUX = 16384
NV = 2048
NT = 2048
NVEC = 64
PARTS = (8, 8)

SIZES = {"xl": 2, "c": 2, "y": 4, "xh": 2, "z": 4}
AXES = tuple(SIZES)
GRP = ("y", "xh", "z")
PANEL = ("xl", "c")
PEERS = ("xl", "y", "xh", "z")


def move(value, axes, target):
    sizes = [SIZES[a] for a in axes]
    total = math.prod(sizes)
    pairs = []
    for source in range(total):
        rest, where = source, {}
        for axis, size in zip(reversed(axes), reversed(sizes)):
            rest, where[axis] = divmod(rest, size)
        there = target(where)
        if there is None:
            continue
        index = 0
        for axis, size in zip(axes, sizes):
            index = index * size + there[axis] % size
        pairs.append((source, index))
    return lax.ppermute(value, axes if len(axes) > 1 else axes[0], pairs)


def shift(value, axis, by):
    return move(value, (axis,), lambda w: {axis: w[axis] + by})


def along(value, by):
    return turn(value, by, 0)


def turn(value, by, x_core):
    def target(w):
        there = dict(w)
        if w["c"] == x_core:
            x = (2 * w["xh"] + w["xl"] + by) % 4
            there["xl"], there["xh"] = x % 2, x // 2
        else:
            there["z"] = w["z"] + by
        return there

    return move(value, ("xl", "c", "xh", "z"), target)


def keeps(w):
    return w["c"] == w["y"] % 2


def to_neighbour_plane(value, by):
    return move(
        value, ("c", "y"), lambda w: None if keeps(w) else {"c": 1 - w["c"], "y": w["y"] + by}
    )


MESSAGE = 1024 + 2 * NVEC


def finish_kernel(table, g0, g1, g2, g3, w_all, bt, proj, out):
    count = out.shape[1]
    pieces = (g0, g1, g2, g3)
    first_core = table[16] == 1

    def on_block(block, coupled):
        rows = pl.multiple_of(block * 256, 256)
        sums = {}
        for g in range(4):
            for u in range(4):
                column = pl.multiple_of(table[4 * g + u] * 512, 512)
                term = lax.dot_general(
                    pieces[g][u],
                    w_all[pl.ds(rows, 256), pl.ds(column, 512)],
                    (((1,), (1,)), ((), ())),
                    preferred_element_type=jnp.float32,
                )
                key = (g % 2, u % 2)
                sums[key] = sums[key] + term if key in sums else term
        mixed = (sums[0, 1], sums[1, 0])
        same = sums[0, 0] + jnp.where(first_core, mixed[1], mixed[0])
        opposite = sums[1, 1] + jnp.where(first_core, mixed[0], mixed[1])
        own = jnp.where(block < 2, 2.0, 0.0)
        same = own * bt[:, pl.ds(pl.multiple_of(lax.rem(rows, 512), 256), 256)].astype(jnp.float32) - same
        added = []
        for slot, part in enumerate((same, -opposite)):
            rounded = part.astype(jnp.bfloat16)
            out[table[17 + slot], :, pl.ds(rows, 256)] = rounded
            added.append(
                coupled[slot]
                + lax.dot_general(
                    rounded,
                    proj[:, pl.ds(rows, 256)],
                    (((1,), (1,)), ((), ())),
                    preferred_element_type=jnp.float32,
                )
            )
        return tuple(added)

    coupled = lax.fori_loop(0, 4, on_block, (jnp.zeros((count, 2 * NVEC), jnp.float32),) * 2)
    high_lanes = lax.broadcasted_iota(jnp.int32, (count, 2 * NVEC), 1) < NVEC
    for slot in range(2):
        high = coupled[slot].astype(jnp.bfloat16).astype(jnp.float32)
        both = jnp.where(high_lanes, high, coupled[slot] - high)
        out[table[17 + slot], :, 1024:] = both.astype(jnp.bfloat16)


def finish_part(table, pieces, w_all, bt, proj):
    count = bt.shape[0]
    in_vmem = pl.BlockSpec(memory_space=pltpu.VMEM)
    return pl.pallas_call(
        finish_kernel,
        out_shape=jax.ShapeDtypeStruct((2, count, MESSAGE), jnp.bfloat16),
        in_specs=[pl.BlockSpec(memory_space=pltpu.SMEM)] + [in_vmem] * 7,
        out_specs=in_vmem,
        compiler_params=pltpu.CompilerParams(vmem_limit_bytes=40 * 2**20),
        cost_estimate=pl.CostEstimate(
            flops=2 * 2 * count * 1024 * 4096, bytes_accessed=14 * 2**20, transcendentals=0
        ),
    )(table, *pieces, w_all, bt, proj)


def after(value, seen):
    ready = jnp.abs(seen[0, 0]) < 1e30
    return jnp.where(ready, value, jnp.zeros_like(value))


def on_device(b_blocks, w_store, owner, trials, eps_occ, eps_virt, slab_first):
    xl, c, y = lax.axis_index("xl"), lax.axis_index("c"), lax.axis_index("y")
    xh, z = lax.axis_index("xh"), lax.axis_index("z")
    parity = lax.rem(y, 2)
    keeper = c == parity
    low = xl == 0
    first_core = c == 0

    starts = [sum(PARTS[:k]) for k in range(len(PARTS))]
    bt = b_blocks.T.reshape(32, 16, 512)
    bt = jnp.concatenate(
        [bt[:, at : at + n].reshape(32 * n, 512) for at, n in zip(starts, PARTS)], axis=0
    )
    from_below, from_above = shift(bt, "y", 1), shift(bt, "y", -1)
    from_across = shift(bt, "y", 2)

    def rows_of(place):
        plane = jnp.sum(jnp.where(owner == place, jnp.arange(4, dtype=jnp.int32), 0))
        off = lax.rem(y - plane + 4, 4)
        return jnp.where(
            off < 2,
            jnp.where(off == 0, bt, from_below),
            jnp.where(off == 2, from_across, from_above),
        )

    mine = rows_of(2 * xl + parity)
    theirs = rows_of(2 * (1 - xl) + parity)
    copies = jnp.broadcast_to(after(trials, shift(bt[:16], "c", 1)), (8,) + trials.shape)
    plane_trials = lax.all_to_all(copies, ("xh", "z"), split_axis=0, concat_axis=0)
    copies = jnp.broadcast_to(plane_trials, (4, 8) + trials.shape)
    trial_rows = lax.all_to_all(copies, "y", split_axis=0, concat_axis=0).reshape(512, NVEC)
    terms = lax.dot_general(
        trial_rows, b_blocks, (((0,), (1,)), ((), ())), preferred_element_type=jnp.float32
    )
    terms = terms + shift(terms, "c", 1)

    load = jnp.concatenate([mine, theirs, terms.astype(jnp.bfloat16)], axis=0)
    p1, p2, p3 = along(load, -1), along(load, 2), along(load, 1)

    seen = shift(load[:16], "c", 1)
    w_lo, w_hi = after(w_store[:256], seen), after(w_store[256:], seen)
    below, above = to_neighbour_plane(w_lo, 1), to_neighbour_plane(w_hi, -1)
    def pick(core0, core1):
        return jnp.where(first_core, core0, core1)

    def gathered(rows):
        own = mine[rows]
        q1, q2, q3 = ((p[:512][rows], p[512:1024][rows]) for p in (p1, p2, p3))
        to_sides = jnp.stack([pick(own, theirs[rows]), q1[1], pick(q2[0], q2[1]), q3[1]])
        to_across = jnp.stack([own, pick(q1[1], q1[0]), q2[0], pick(q3[1], q3[0])])
        return [to_across, turn(to_sides, -1, 1), turn(to_across, 2, 1), turn(to_sides, 1, 1)]

    starts_at = [32 * at for at in starts]
    gathered_parts = [
        gathered(slice(at, at + 32 * n)) for at, n in zip(starts_at, PARTS)
    ]
    seen = shift(gathered_parts[0][0][0, :16], "c", 1)
    swap_lo = shift(after(jnp.where(keeper, w_lo, below), seen), "c", 1)
    swap_hi = shift(after(jnp.where(keeper, w_hi, above), seen), "c", 1)
    w_all = jnp.concatenate(
        [
            jnp.where(keeper, w_lo, swap_lo),
            jnp.where(keeper, w_hi, swap_hi),
            jnp.where(keeper, swap_lo, below),
            jnp.where(keeper, swap_hi, above),
        ],
        axis=0,
    )

    from_pair = after(jnp.where(low, p1[1024:], p3[1024:]), seen)
    from_pair = pick(from_pair, shift(from_pair, "c", 1))
    proj = (terms + from_pair.astype(jnp.float32)).astype(jnp.bfloat16)
    proj = jnp.concatenate([proj, proj], axis=0)
    proj_rows = jnp.concatenate(
        [proj, shift(proj[:, :256], "y", 1), shift(proj[:, 256:], "y", -1)], axis=1
    )

    columns = []
    for g in range(4):
        for u in range(4):
            options = []
            for x_off, z_off in ((u, g), (g, u)):
                far = (0, 1 - low.astype(jnp.int32), 1, low.astype(jnp.int32))[x_off]
                options.append(jnp.where(far == 0, xh, 1 - xh) * 4 + lax.rem(z + z_off, 4))
            columns.append(pick(*options))
    table = jnp.stack(columns + [1 - c, xl, 1 - xl])

    def finish(pieces, at, n):
        out = finish_part(table, pieces, w_all, bt[32 * at : 32 * (at + n)], proj_rows)
        got = lax.all_to_all(out.reshape(64, n, MESSAGE), PEERS, split_axis=0, concat_axis=0)
        got = got.astype(jnp.float32).reshape(2, 4, 8, n, MESSAGE).sum(axis=0)
        first = jnp.roll(got[..., 512:768], -1, axis=0)
        second = jnp.roll(got[..., 768:1024], 1, axis=0)
        kernel = got[..., :512] + jnp.concatenate([first, second], axis=-1)
        kernel = kernel.astype(jnp.bfloat16).transpose(2, 0, 1, 3).reshape(n, NAUX)
        return kernel, jnp.sum(got[..., 1024:1088] + got[..., 1088:], axis=(0, 1))

    parts = [finish(*part) for part in zip(gathered_parts, starts, PARTS)]
    kernel_rows = jnp.concatenate([k for k, _ in parts], axis=0)
    coupling = jnp.concatenate([v for _, v in parts], axis=0)

    rows_here = 16
    first_row = ((xl * 2 + c) * 32 + y * 8 + xh * 4 + z) * rows_here
    occ_index = slab_first[0] + first_row // NV
    positions = jnp.arange(eps_occ.shape[0], dtype=jnp.int32)
    occupied = jnp.sum(jnp.where(positions == occ_index, eps_occ, 0.0))
    virtual = lax.dynamic_slice_in_dim(eps_virt, first_row % NV, rows_here, 0)
    diagonal = (virtual - occupied)[:, None]
    sigma = diagonal * trials.astype(jnp.float32) + coupling * (1.0 / math.sqrt(NAUX * NT))
    return (kernel_rows, sigma)


def solution(mesh):
    fine = Mesh(mesh.devices.reshape(tuple(SIZES.values())), AXES)
    in_specs = (P(GRP, PANEL), P(GRP, PANEL), P(), P(PANEL + GRP, None), P(), P(), P())
    out_specs = (P(PANEL + GRP, None), P(PANEL + GRP, None))
    return jax.shard_map(
        on_device, mesh=fine, in_specs=in_specs, out_specs=out_specs, check_vma=False
    )
```

time: 224 us -> 186 us (0.83)
  the two profiles are of different devices: /device:TPU:1 before, /device:TPU:0 now
where the time goes in v2:
time: 186 us; the launch traced here: 185 us
  waiting for transfers between devices  71 us (38%)
  starting transfers between devices  59.5 us (32%)
  other arithmetic  24.7 us (13%)
  Pallas kernels  15.9 us (9%)
  local copies, waits for them, and re-layouts  8.22 us (4%)
  between operations  5.07 us (3%)
    ppermute x23, waiting for transfers between devices, move(): return lax.ppermute(value, axes if len(axes) > 1 else axes[0], pairs)  40.4 us
    ppermute x23, starting transfers between devices, move(): return lax.ppermute(value, axes if len(axes) > 1 else axes[0], pairs)  29.3 us
    all_to_all x2, waiting for transfers between devices, finish(): lax.all_to_all(out.reshape(64, n, MESSAGE), PEERS, split_axis=0, concat_a...  19.4 us
    all_to_all x2, starting transfers between devices, finish(): lax.all_to_all(out.reshape(64, n, MESSAGE), PEERS, split_axis=0, concat_a...  19.2 us
    pallas_call x2, Pallas kernels, finish_part(): pl.pallas_call(finish_kernel, out_shape=jax.ShapeDtypeStruct((2, count, M...  15.9 us
    all_to_all x1, starting transfers between devices, on_device(): lax.all_to_all(copies, ('xh', 'z'), split_axis=0, concat_axis=0)  7.77 us
    all_to_all x1, waiting for transfers between devices, on_device(): lax.all_to_all(copies, ('xh', 'z'), split_axis=0, concat_axis=0)  7.72 us
    select_n x5, other arithmetic, after(): return jnp.where(ready, value, jnp.zeros_like(value))  6.8 us
  transfers between devices with their start and end apart: 27, of which 11 were waited for; matrix products, arithmetic and copies ran while one was open for 13% of the time, Pallas kernels for 9%

profile of v2, /device:TPU:0, one launch (start us, length us, event | category | flops | bytes accessed | tf_op | source)
XLA Modules:
  0.0 184.7 jit_solution(2892992630892219974)
XLA Ops:
  0.7 1.3 copy.12
  2.1 0.8 pad_maximum_fusion.6
  2.9 1.7 collective-permute-start
  4.6 2.9 %collective-permute-start.1 = (bf16[512,512]{1,0:T(8,128)(2,1)}, bf16[512,512]{1,0:T(8,128)(2,1)S(1)}, u32[]{:S(2)}, u32[]{:S(2)}) collective-permute-start(bf16[512,512]{1,0:T(8,128)(2,1)} %pad_maximum_fusion.6), channel_id=1, source_target_pairs={{0,16},{8,24},{16,0},{24,8},{1,17},{9,25},{17,1},{25,9},{2,18},{10... | collective-permute-start | bytes 1572872 | tf_op jit(solution)/shard_map/ppermute | solution.py:39
  7.5 1.3 collective-permute-start.2
  10.8 7.8 %all-to-all-start = ((bf16[8,2,512]{2,1,0:T(2,128)(2,1)}), bf16[8,2,512]{2,1,0:T(2,128)(2,1)S(1)}, u32[]{:S(2)}, u32[]{:S(2)}) async-start(bf16[8,2,512]{2,1,0:T(2,128)(2,1)} %reshape.67), calls=%async_computation | async-start | bytes 32768 | tf_op jit(solution)/shard_map/all_to_all | solution.py:171
  18.5 7.7 %all-to-all-done = bf16[8,2,512]{2,1,0:T(2,128)(2,1)S(1)} async-done(((bf16[8,2,512]{2,1,0:T(2,128)(2,1)}), bf16[8,2,512]{2,1,0:T(2,128)(2,1)S(1)}, u32[]{:S(2)}, u32[]{:S(2)}) %all-to-all-start) | async-done | bytes 16416 | tf_op jit(solution)/shard_map/all_to_all | solution.py:171
  26.4 0.8 reshape.69
  27.2 3.3 %all-to-all-start.1 = ((bf16[4,2,4096]{2,1,0:T(2,128)(2,1)}), bf16[4,2,4096]{2,1,0:T(2,128)(2,1)S(1)}, u32[]{:S(2)}, u32[]{:S(2)}) async-start(bf16[4,2,4096]{2,1,0:T(2,128)(2,1)} %reshape.69), calls=%async_computation.1 | async-start | bytes 131072 | tf_op jit(solution)/shard_map/all_to_all | solution.py:173
  32.5 3.6 %all-to-all-done.1 = bf16[4,2,4096]{2,1,0:T(2,128)(2,1)S(1)} async-done(((bf16[4,2,4096]{2,1,0:T(2,128)(2,1)}), bf16[4,2,4096]{2,1,0:T(2,128)(2,1)S(1)}, u32[]{:S(2)}, u32[]{:S(2)}) %all-to-all-start.1) | async-done | bytes 65568 | tf_op jit(solution)/shard_map/all_to_all | solution.py:173
  39.8 2.3 %slice_select_fusion.1 = (bf16[256,4096]{1,0:T(8,128)(2,1)}, bf16[256,4096]{1,0:T(8,128)(2,1)}) fusion(bf16[512,4096]{1,0:T(8,128)(2,1)S(1)} %copy-done.2, pred[]{:T(512)} %bitcast.35), kind=kLoop, calls=%fused_computation.6 | loop fusion | flops 2097152 | bytes 8388609 | tf_op jit(solution)/shard_map/jit(_where)/select_n | solution.py:140
  42.1 2.0 %collective-permute-start.13 = (bf16[256,4096]{1,0:T(8,128)(2,1)}, bf16[256,4096]{1,0:T(8,128)(2,1)}, u32[]{:S(2)}, u32[]{:S(2)}) collective-permute-start(bf16[256,4096]{1,0:T(8,128)(2,1)} %get-tuple-element.6), channel_id=1, source_target_pairs={{8,48},{24,32},{32,8},{48,24},{9,49},{25,33},{33,9},{49,25},{10,50... | collective-permute-start | bytes 6291464 | tf_op jit(solution)/shard_map/ppermute | solution.py:39
  44.1 1.1 pad_maximum_fusion.1
  45.5 1.7 collective-permute-start.7
  47.2 0.8 fusion.7
  48.0 2.1 %collective-permute-start.15 = (bf16[256,4096]{1,0:T(8,128)(2,1)}, bf16[256,4096]{1,0:T(8,128)(2,1)}, u32[]{:S(2)}, u32[]{:S(2)}) collective-permute-start(bf16[256,4096]{1,0:T(8,128)(2,1)} %get-tuple-element.7), channel_id=1, source_target_pairs={{8,32},{24,48},{32,24},{48,8},{9,33},{25,49},{33,25},{49,9},{10,34... | collective-permute-start | bytes 6291464 | tf_op jit(solution)/shard_map/ppermute | solution.py:39
  50.1 2.9 %collective-permute-start.12 = (bf16[16,512]{1,0:T(8,128)(2,1)S(1)}, bf16[16,512]{1,0:T(8,128)(2,1)S(1)}, u32[]{:S(2)}, u32[]{:S(2)}) collective-permute-start(bf16[16,512]{1,0:T(8,128)(2,1)S(1)} %slice_bitcast_fusion.10), channel_id=1, source_target_pairs={{0,32},{32,0},{1,33},{33,1},{2,34},{34,2},{3,35},{35,3},{4,36},{36... | collective-permute-start | bytes 49160 | tf_op jit(solution)/shard_map/ppermute | solution.py:39
  53.1 0.7 collective-permute-done.12
  55.6 5.4 %collective-permute-done.5 = bf16[1088,512]{1,0:T(8,128)(2,1)} collective-permute-done((bf16[1088,512]{1,0:T(8,128)(2,1)}, bf16[1088,512]{1,0:T(8,128)(2,1)}, u32[]{:S(2)}, u32[]{:S(2)}) %collective-permute-start.5) | collective-permute-done | bytes 1114144 | tf_op jit(solution)/shard_map/ppermute | solution.py:39
  61.0 13.4 %collective-permute-done.7 = bf16[1088,512]{1,0:T(8,128)(2,1)S(1)} collective-permute-done((bf16[1088,512]{1,0:T(8,128)(2,1)}, bf16[1088,512]{1,0:T(8,128)(2,1)S(1)}, u32[]{:S(2)}, u32[]{:S(2)}) %collective-permute-start.7) | collective-permute-done | bytes 1114144 | tf_op jit(solution)/shard_map/ppermute | solution.py:39
  74.4 0.9 fusion.13
  75.4 1.3 slice_bitcast_fusion.8
  76.8 1.8 select_select_fusion.1
  79.2 1.9 %select_select_fusion = bf16[256,4096]{1,0:T(8,128)(2,1)S(1)} fusion(bf16[256,4096]{1,0:T(8,128)(2,1)} %get-tuple-element.7, bf16[256,4096]{1,0:T(8,128)(2,1)} %collective-permute-done.15, pred[]{:T(512)} %bitcast.37, pred[]{:T(512)S(6)} %eq.73), kind=kLoop, calls=%fused_computation.3 | loop fusion | flops 2097152 | bytes 6291458 | tf_op jit(solution)/shard_map/jit(_where)/select_n | solution.py:140
  82.1 1.2 pad_maximum_fusion.5
  83.3 1.7 collective-permute-start.18
  85.0 1.6 collective-permute-start.19
  86.7 2.6 %collective-permute-done.18 = bf16[128,256]{1,0:T(8,128)(2,1)S(1)} collective-permute-done((bf16[128,256]{1,0:T(8,128)(2,1)S(1)}, bf16[128,256]{1,0:T(8,128)(2,1)S(1)}, u32[]{:S(2)}, u32[]{:S(2)}) %collective-permute-start.18) | collective-permute-done | bytes 65568 | tf_op jit(solution)/shard_map/ppermute | solution.py:39
  89.3 2.3 %collective-permute-start.8 = (bf16[4,256,512]{2,1,0:T(8,128)(2,1)S(1)}, bf16[4,256,512]{2,1,0:T(8,128)(2,1)S(1)}, u32[]{:S(2)}, u32[]{:S(2)}) collective-permute-start(bf16[4,256,512]{2,1,0:T(8,128)(2,1)S(1)} %pad_maximum_fusion.3), channel_id=1, source_target_pairs={{0,3},{1,0},{2,1},{3,2},{4,7},{5,4},{6,5},{7,6},{32,100},{33,101},... | collective-permute-start | bytes 3145736 | tf_op jit(solution)/shard_map/ppermute | solution.py:39
  91.6 1.1 collective-permute-start.20
  92.7 1.0 collective-permute-start.22
  93.7 1.9 %broadcast_select_fusion.3 = (bf16[256,4096]{1,0:T(8,128)(2,1)S(1)}, bf16[256,4096]{1,0:T(8,128)(2,1)S(1)}) fusion(bf16[256,4096]{1,0:T(8,128)(2,1)} %get-tuple-element.6, bf16[256,4096]{1,0:T(8,128)(2,1)S(1)} %collective-permute-done.14, pred[]{:T(512)S(6)} %eq.73, bf16[256,4096]{1,0:T(8,128)(2,1)} %collective-permute-done.13), kind=kLoop, calls=%fused_computation.10 | loop fusion | flops 2097152 | bytes 10485761 | tf_op jit(solution)/shard_map/jit(_where)/select_n | solution.py:204
  95.7 1.3 collective-permute-start.9
  97.0 1.9 %broadcast_select_fusion.2 = (bf16[256,4096]{1,0:T(8,128)(2,1)S(1)}, bf16[256,4096]{1,0:T(8,128)(2,1)S(1)}) fusion(bf16[256,4096]{1,0:T(8,128)(2,1)} %get-tuple-element.7, bf16[256,4096]{1,0:T(8,128)(2,1)S(1)} %collective-permute-done.16, pred[]{:T(512)S(6)} %eq.73, bf16[256,4096]{1,0:T(8,128)(2,1)} %collective-permute-done.15), kind=kLoop, calls=%fused_computation.9 | loop fusion | flops 2097152 | bytes 10485761 | tf_op jit(solution)/shard_map/jit(_where)/select_n | solution.py:205
  99.0 1.1 pad_maximum_fusion.w_all
  100.0 2.5 %collective-permute-start.21 = (bf16[4,256,512]{2,1,0:T(8,128)(2,1)S(1)}, bf16[4,256,512]{2,1,0:T(8,128)(2,1)}, u32[]{:S(2)}, u32[]{:S(2)}) collective-permute-start(bf16[4,256,512]{2,1,0:T(8,128)(2,1)S(1)} %pad_maximum_fusion.4.g0), channel_id=1, source_target_pairs={{0,2},{1,3},{2,0},{3,1},{4,6},{5,7},{6,4},{7,5},{32,36},{33,37},{3... | collective-permute-start | bytes 3145736 | tf_op jit(solution)/shard_map/ppermute | solution.py:39
  102.6 1.6 collective-permute-done.8.g1
  104.1 16.3 %collective-permute-done.9.g2 = bf16[4,256,512]{2,1,0:T(8,128)(2,1)S(1)} collective-permute-done((bf16[4,256,512]{2,1,0:T(8,128)(2,1)S(1)}, bf16[4,256,512]{2,1,0:T(8,128)(2,1)S(1)}, u32[]{:S(2)}, u32[]{:S(2)}) %collective-permute-start.9) | collective-permute-done | bytes 1048608 | tf_op jit(solution)/shard_map/ppermute | solution.py:39
  120.5 7.4 %shard_map.86 = bf16[2,256,1152]{2,1,0:T(8,128)(2,1)} custom-call(s32[19]{0:T(128)S(1)} %stack.139.table, bf16[4,256,512]{2,1,0:T(8,128)(2,1)S(1)} %pad_maximum_fusion.2.g0, bf16[4,256,512]{2,1,0:T(8,128)(2,1)S(1)} %collective-permute-done.8.g1, bf16[4,256,512]{2,1,0:T(8,128)(2,1)S(1)} %collective-permute-done.9.g2, ...), custom_call_target="tpu_custom_call" | custom-call | flops 4294967296 | bytes 14680064 | tf_op jit(solution)/shard_map/pallas_call | solution.py:126
  127.8 13.6 %all-to-all-start.2 = ((bf16[64,8,1152]{2,1,0:T(8,128)(2,1)}), bf16[64,8,1152]{2,1,0:T(8,128)(2,1)}, u32[]{:S(2)}, u32[]{:S(2)}) async-start(bf16[64,8,1152]{2,1,0:T(8,128)(2,1)} %bitcast.38), calls=%async_computation.2 | async-start | bytes 2359296 | tf_op jit(solution)/shard_map/all_to_all | solution.py:232
  141.5 3.4 %copy-done.1 = bf16[1024,4096]{1,0:T(8,128)(2,1)S(1)} copy-done((bf16[1024,4096]{1,0:T(8,128)(2,1)S(1)}, bf16[1024,4096]{1,0:T(8,128)(2,1)}, u32[]{:S(2)}) %copy-start.1) | copy-done | bytes 8388632
  144.8 8.5 %shard_map.87 = bf16[2,256,1152]{2,1,0:T(8,128)(2,1)} custom-call(s32[19]{0:T(128)S(1)} %stack.139.table, bf16[4,256,512]{2,1,0:T(8,128)(2,1)S(1)} %pad_maximum_fusion.4.g0, bf16[4,256,512]{2,1,0:T(8,128)(2,1)S(1)} %collective-permute-done.20.g1, bf16[4,256,512]{2,1,0:T(8,128)(2,1)} %collective-permute-done.21.g2, ...), custom_call_target="tpu_custom_call" | custom-call | flops 4294967296 | bytes 14680064 | tf_op jit(solution)/shard_map/pallas_call | solution.py:126
  153.3 6.0 %all-to-all-done.2 = bf16[64,8,1152]{2,1,0:T(8,128)(2,1)} async-done(((bf16[64,8,1152]{2,1,0:T(8,128)(2,1)}), bf16[64,8,1152]{2,1,0:T(8,128)(2,1)}, u32[]{:S(2)}, u32[]{:S(2)}) %all-to-all-start.2) | async-done | bytes 1179680 | tf_op jit(solution)/shard_map/all_to_all | solution.py:232
  159.4 5.6 %all-to-all-start.3 = ((bf16[64,8,1152]{2,1,0:T(8,128)(2,1)}), bf16[64,8,1152]{2,1,0:T(8,128)(2,1)S(1)}, u32[]{:S(2)}, u32[]{:S(2)}) async-start(bf16[64,8,1152]{2,1,0:T(8,128)(2,1)} %bitcast.50), calls=%async_computation.3 | async-start | bytes 2359296 | tf_op jit(solution)/shard_map/all_to_all | solution.py:232
  166.3 1.4 dynamic-slice_subtract_fusion
  167.7 1.6 convert_reduce_fusion.1
  169.3 13.3 %all-to-all-done.3 = bf16[64,8,1152]{2,1,0:T(8,128)(2,1)S(1)} async-done(((bf16[64,8,1152]{2,1,0:T(8,128)(2,1)}), bf16[64,8,1152]{2,1,0:T(8,128)(2,1)S(1)}, u32[]{:S(2)}, u32[]{:S(2)}) %all-to-all-start.3) | async-done | bytes 1179680 | tf_op jit(solution)/shard_map/all_to_all | solution.py:232
  183.2 0.8 pad_maximum_fusion.7
  (79 shorter events, 10.6 us)
Async XLA Ops:
  0.6 35.6 %copy-start.3 = (bf16[512,512]{1,0:T(8,128)(2,1)S(1)}, bf16[512,512]{1,0:T(8,128)(2,1)}, u32[]{:S(2)}) copy-start(bf16[512,512]{1,0:T(8,128)(2,1)} %param.7) | copy-start | bytes 1572868
  0.6 9.4 %copy-start.6 = (bf16[16,64]{1,0:T(8,128)(2,1)S(1)}, bf16[16,64]{1,0:T(8,128)(2,1)}, u32[]{:S(2)}) copy-start(bf16[16,64]{1,0:T(8,128)(2,1)} %param.10) | copy-start | bytes 6148
  0.6 29.8 %copy-start.7 = (s32[4]{0:T(128)S(1)}, s32[4]{0:T(128)}, u32[]{:S(2)}) copy-start(s32[4]{0:T(128)} %param.9) | copy-start | bytes 52
  2.0 6.9 %collective-permute-start.3 = (bf16[16,512]{1,0:T(8,128)(2,1)S(1)}, bf16[16,512]{1,0:T(8,128)(2,1)S(1)}, u32[]{:S(2)}, u32[]{:S(2)}) collective-permute-start(bf16[16,512]{1,0:T(8,128)(2,1)S(1)} %slice_bitcast_fusion.11), channel_id=1, source_target_pairs={{0,32},{32,0},{1,33},{33,1},{2,34},{34,2},{3,35},{35,3},{4,36},{36... | collective-permute-start | bytes 49160 | tf_op jit(solution)/shard_map/ppermute | solution.py:39
  2.9 33.7 %collective-permute-start = (bf16[512,512]{1,0:T(8,128)(2,1)}, bf16[512,512]{1,0:T(8,128)(2,1)S(1)}, u32[]{:S(2)}, u32[]{:S(2)}) collective-permute-start(bf16[512,512]{1,0:T(8,128)(2,1)} %pad_maximum_fusion.6), channel_id=1, source_target_pairs={{0,8},{8,16},{16,24},{24,0},{1,9},{9,17},{17,25},{25,1},{2,10},{10... | collective-permute-start | bytes 1572872 | tf_op jit(solution)/shard_map/ppermute | solution.py:39
  4.6 32.0 %collective-permute-start.1 = (bf16[512,512]{1,0:T(8,128)(2,1)}, bf16[512,512]{1,0:T(8,128)(2,1)S(1)}, u32[]{:S(2)}, u32[]{:S(2)}) collective-permute-start(bf16[512,512]{1,0:T(8,128)(2,1)} %pad_maximum_fusion.6), channel_id=1, source_target_pairs={{0,16},{8,24},{16,0},{24,8},{1,17},{9,25},{17,1},{25,9},{2,18},{10... | collective-permute-start | bytes 1572872 | tf_op jit(solution)/shard_map/ppermute | solution.py:39
  7.5 29.1 %collective-permute-start.2 = (bf16[512,512]{1,0:T(8,128)(2,1)}, bf16[512,512]{1,0:T(8,128)(2,1)S(1)}, u32[]{:S(2)}, u32[]{:S(2)}) collective-permute-start(bf16[512,512]{1,0:T(8,128)(2,1)} %pad_maximum_fusion.6), channel_id=1, source_target_pairs={{0,24},{8,0},{16,8},{24,16},{1,25},{9,1},{17,9},{25,17},{2,26},{10... | collective-permute-start | bytes 1572872 | tf_op jit(solution)/shard_map/ppermute | solution.py:39
  10.8 15.5 %all-to-all-start = ((bf16[8,2,512]{2,1,0:T(2,128)(2,1)}), bf16[8,2,512]{2,1,0:T(2,128)(2,1)S(1)}, u32[]{:S(2)}, u32[]{:S(2)}) async-start(bf16[8,2,512]{2,1,0:T(2,128)(2,1)} %reshape.67), calls=%async_computation | async-start | bytes 32768 | tf_op jit(solution)/shard_map/all_to_all | solution.py:171
  27.2 8.9 %all-to-all-start.1 = ((bf16[4,2,4096]{2,1,0:T(2,128)(2,1)}), bf16[4,2,4096]{2,1,0:T(2,128)(2,1)S(1)}, u32[]{:S(2)}, u32[]{:S(2)}) async-start(bf16[4,2,4096]{2,1,0:T(2,128)(2,1)} %reshape.69), calls=%async_computation.1 | async-start | bytes 131072 | tf_op jit(solution)/shard_map/all_to_all | solution.py:173
  36.2 3.6 %copy-start.2 = (bf16[512,4096]{1,0:T(8,128)(2,1)S(1)}, bf16[512,4096]{1,0:T(8,128)(2,1)}, u32[]{:S(2)}) copy-start(bf16[512,4096]{1,0:T(8,128)(2,1)} %param.8) | copy-start | bytes 12582916
  36.5 1.4 collective-permute-start.4
  37.0 1.6 collective-permute-start.11
  42.1 34.7 %collective-permute-start.13 = (bf16[256,4096]{1,0:T(8,128)(2,1)}, bf16[256,4096]{1,0:T(8,128)(2,1)}, u32[]{:S(2)}, u32[]{:S(2)}) collective-permute-start(bf16[256,4096]{1,0:T(8,128)(2,1)} %get-tuple-element.6), channel_id=1, source_target_pairs={{8,48},{24,32},{32,8},{48,24},{9,49},{25,33},{33,9},{49,25},{10,50... | collective-permute-start | bytes 6291464 | tf_op jit(solution)/shard_map/ppermute | solution.py:39
  45.2 15.8 %collective-permute-start.5 = (bf16[1088,512]{1,0:T(8,128)(2,1)}, bf16[1088,512]{1,0:T(8,128)(2,1)}, u32[]{:S(2)}, u32[]{:S(2)}) collective-permute-start(bf16[1088,512]{1,0:T(8,128)(2,1)} %pad_maximum_fusion.1), channel_id=1, source_target_pairs={{0,68},{1,69},{2,70},{3,71},{4,64},{5,65},{6,66},{7,67},{32,35},{3... | collective-permute-start | bytes 3342344 | tf_op jit(solution)/shard_map/ppermute | solution.py:39
  45.5 28.9 %collective-permute-start.7 = (bf16[1088,512]{1,0:T(8,128)(2,1)}, bf16[1088,512]{1,0:T(8,128)(2,1)S(1)}, u32[]{:S(2)}, u32[]{:S(2)}) collective-permute-start(bf16[1088,512]{1,0:T(8,128)(2,1)} %pad_maximum_fusion.1), channel_id=1, source_target_pairs={{0,64},{1,65},{2,66},{3,67},{4,68},{5,69},{6,70},{7,71},{32,33},{3... | collective-permute-start | bytes 3342344 | tf_op jit(solution)/shard_map/ppermute | solution.py:39
  48.0 31.2 %collective-permute-start.15 = (bf16[256,4096]{1,0:T(8,128)(2,1)}, bf16[256,4096]{1,0:T(8,128)(2,1)}, u32[]{:S(2)}, u32[]{:S(2)}) collective-permute-start(bf16[256,4096]{1,0:T(8,128)(2,1)} %get-tuple-element.7), channel_id=1, source_target_pairs={{8,32},{24,48},{32,24},{48,8},{9,33},{25,49},{33,25},{49,9},{10,34... | collective-permute-start | bytes 6291464 | tf_op jit(solution)/shard_map/ppermute | solution.py:39
  50.1 3.8 %collective-permute-start.12 = (bf16[16,512]{1,0:T(8,128)(2,1)S(1)}, bf16[16,512]{1,0:T(8,128)(2,1)S(1)}, u32[]{:S(2)}, u32[]{:S(2)}) collective-permute-start(bf16[16,512]{1,0:T(8,128)(2,1)S(1)} %slice_bitcast_fusion.10), channel_id=1, source_target_pairs={{0,32},{32,0},{1,33},{33,1},{2,34},{34,2},{3,35},{35,3},{4,36},{36... | collective-permute-start | bytes 49160 | tf_op jit(solution)/shard_map/ppermute | solution.py:39
  53.8 25.3 %collective-permute-start.6 = (bf16[1088,512]{1,0:T(8,128)(2,1)}, bf16[1088,512]{1,0:T(8,128)(2,1)S(1)}, u32[]{:S(2)}, u32[]{:S(2)}) collective-permute-start(bf16[1088,512]{1,0:T(8,128)(2,1)} %pad_maximum_fusion.1), channel_id=1, source_target_pairs={{0,4},{1,5},{2,6},{3,7},{4,0},{5,1},{6,2},{7,3},{32,34},{33,35},{3... | collective-permute-start | bytes 3342344 | tf_op jit(solution)/shard_map/ppermute | solution.py:39
  75.2 8.0 %collective-permute-start.17 = (bf16[64,512]{1,0:T(8,128)(2,1)S(1)}, bf16[64,512]{1,0:T(8,128)(2,1)S(1)}, u32[]{:S(2)}, u32[]{:S(2)}) collective-permute-start(bf16[64,512]{1,0:T(8,128)(2,1)S(1)} %fusion.13), channel_id=1, source_target_pairs={{0,32},{32,0},{1,33},{33,1},{2,34},{34,2},{3,35},{35,3},{4,36},{36... | collective-permute-start | bytes 196616 | tf_op jit(solution)/shard_map/ppermute | solution.py:39
  78.6 14.1 %collective-permute-start.14 = (bf16[256,4096]{1,0:T(8,128)(2,1)S(1)}, bf16[256,4096]{1,0:T(8,128)(2,1)S(1)}, u32[]{:S(2)}, u32[]{:S(2)}) collective-permute-start(bf16[256,4096]{1,0:T(8,128)(2,1)S(1)} %select_select_fusion.1), channel_id=1, source_target_pairs={{0,32},{32,0},{1,33},{33,1},{2,34},{34,2},{3,35},{35,3},{4,36},{36... | collective-permute-start | bytes 6291464 | tf_op jit(solution)/shard_map/ppermute | solution.py:39
  79.2 2.1 %copy-start.4 = (bf16[1,256,512]{2,1,0:T(8,128)(2,1)S(1)}, bf16[1,256,512]{2,1,0:T(8,128)(2,1)}, u32[]{:S(2)}) copy-start(bf16[1,256,512]{2,1,0:T(8,128)(2,1)} %get-tuple-element.34) | copy-start | bytes 786436
  81.0 14.6 %collective-permute-start.16 = (bf16[256,4096]{1,0:T(8,128)(2,1)S(1)}, bf16[256,4096]{1,0:T(8,128)(2,1)S(1)}, u32[]{:S(2)}, u32[]{:S(2)}) collective-permute-start(bf16[256,4096]{1,0:T(8,128)(2,1)S(1)} %select_select_fusion), channel_id=1, source_target_pairs={{0,32},{32,0},{1,33},{33,1},{2,34},{34,2},{3,35},{35,3},{4,36},{36... | collective-permute-start | bytes 6291464 | tf_op jit(solution)/shard_map/ppermute | solution.py:39
  81.4 18.7 %collective-permute-start.10 = (bf16[4,256,512]{2,1,0:T(8,128)(2,1)S(1)}, bf16[4,256,512]{2,1,0:T(8,128)(2,1)S(1)}, u32[]{:S(2)}, u32[]{:S(2)}) collective-permute-start(bf16[4,256,512]{2,1,0:T(8,128)(2,1)S(1)} %pad_maximum_fusion.3), channel_id=1, source_target_pairs={{0,1},{1,2},{2,3},{3,0},{4,5},{5,6},{6,7},{7,4},{32,96},{33,97},{3... | collective-permute-start | bytes 3145736 | tf_op jit(solution)/shard_map/ppermute | solution.py:39
  81.9 1.3 copy-start.5
  83.3 6.0 %collective-permute-start.18 = (bf16[128,256]{1,0:T(8,128)(2,1)S(1)}, bf16[128,256]{1,0:T(8,128)(2,1)S(1)}, u32[]{:S(2)}, u32[]{:S(2)}) collective-permute-start(bf16[128,256]{1,0:T(8,128)(2,1)S(1)} %get-tuple-element.40), channel_id=1, source_target_pairs={{0,8},{8,16},{16,24},{24,0},{1,9},{9,17},{17,25},{25,1},{2,10},{10... | collective-permute-start | bytes 196616 | tf_op jit(solution)/shard_map/ppermute | solution.py:39
  85.0 6.6 %collective-permute-start.19 = (bf16[128,256]{1,0:T(8,128)(2,1)S(1)}, bf16[128,256]{1,0:T(8,128)(2,1)S(1)}, u32[]{:S(2)}, u32[]{:S(2)}) collective-permute-start(bf16[128,256]{1,0:T(8,128)(2,1)S(1)} %get-tuple-element.41), channel_id=1, source_target_pairs={{0,24},{8,0},{16,8},{24,16},{1,25},{9,1},{17,9},{25,17},{2,26},{10... | collective-permute-start | bytes 196616 | tf_op jit(solution)/shard_map/ppermute | solution.py:39
  89.3 14.8 %collective-permute-start.8 = (bf16[4,256,512]{2,1,0:T(8,128)(2,1)S(1)}, bf16[4,256,512]{2,1,0:T(8,128)(2,1)S(1)}, u32[]{:S(2)}, u32[]{:S(2)}) collective-permute-start(bf16[4,256,512]{2,1,0:T(8,128)(2,1)S(1)} %pad_maximum_fusion.3), channel_id=1, source_target_pairs={{0,3},{1,0},{2,1},{3,2},{4,7},{5,4},{6,5},{7,6},{32,100},{33,101},... | collective-permute-start | bytes 3145736 | tf_op jit(solution)/shard_map/ppermute | solution.py:39
  91.6 49.8 %collective-permute-start.20 = (bf16[4,256,512]{2,1,0:T(8,128)(2,1)}, bf16[4,256,512]{2,1,0:T(8,128)(2,1)S(1)}, u32[]{:S(2)}, u32[]{:S(2)}) collective-permute-start(bf16[4,256,512]{2,1,0:T(8,128)(2,1)} %pad_maximum_fusion.5), channel_id=1, source_target_pairs={{0,3},{1,0},{2,1},{3,2},{4,7},{5,4},{6,5},{7,6},{32,100},{33,101},... | collective-permute-start | bytes 3145736 | tf_op jit(solution)/shard_map/ppermute | solution.py:39
  92.7 48.7 %collective-permute-start.22 = (bf16[4,256,512]{2,1,0:T(8,128)(2,1)}, bf16[4,256,512]{2,1,0:T(8,128)(2,1)}, u32[]{:S(2)}, u32[]{:S(2)}) collective-permute-start(bf16[4,256,512]{2,1,0:T(8,128)(2,1)} %pad_maximum_fusion.5), channel_id=1, source_target_pairs={{0,1},{1,2},{2,3},{3,0},{4,5},{5,6},{6,7},{7,4},{32,96},{33,97},{3... | collective-permute-start | bytes 3145736 | tf_op jit(solution)/shard_map/ppermute | solution.py:39
  95.7 24.8 %collective-permute-start.9 = (bf16[4,256,512]{2,1,0:T(8,128)(2,1)S(1)}, bf16[4,256,512]{2,1,0:T(8,128)(2,1)S(1)}, u32[]{:S(2)}, u32[]{:S(2)}) collective-permute-start(bf16[4,256,512]{2,1,0:T(8,128)(2,1)S(1)} %pad_maximum_fusion.2.g0), channel_id=1, source_target_pairs={{0,2},{1,3},{2,0},{3,1},{4,6},{5,7},{6,4},{7,5},{32,36},{33,37},{3... | collective-permute-start | bytes 3145736 | tf_op jit(solution)/shard_map/ppermute | solution.py:39
  100.0 27.8 %copy-start = (bf16[1024,4096]{1,0:T(8,128)(2,1)}, bf16[1024,4096]{1,0:T(8,128)(2,1)S(1)}, u32[]{:S(2)}) copy-start(bf16[1024,4096]{1,0:T(8,128)(2,1)S(1)} %pad_maximum_fusion.w_all) | copy-start | bytes 25165828
  100.0 41.4 %collective-permute-start.21 = (bf16[4,256,512]{2,1,0:T(8,128)(2,1)S(1)}, bf16[4,256,512]{2,1,0:T(8,128)(2,1)}, u32[]{:S(2)}, u32[]{:S(2)}) collective-permute-start(bf16[4,256,512]{2,1,0:T(8,128)(2,1)S(1)} %pad_maximum_fusion.4.g0), channel_id=1, source_target_pairs={{0,2},{1,3},{2,0},{3,1},{4,6},{5,7},{6,4},{7,5},{32,36},{33,37},{3... | collective-permute-start | bytes 3145736 | tf_op jit(solution)/shard_map/ppermute | solution.py:39
  127.8 31.5 %all-to-all-start.2 = ((bf16[64,8,1152]{2,1,0:T(8,128)(2,1)}), bf16[64,8,1152]{2,1,0:T(8,128)(2,1)}, u32[]{:S(2)}, u32[]{:S(2)}) async-start(bf16[64,8,1152]{2,1,0:T(8,128)(2,1)} %bitcast.38), calls=%async_computation.2 | async-start | bytes 2359296 | tf_op jit(solution)/shard_map/all_to_all | solution.py:232
  141.4 3.4 %copy-start.1 = (bf16[1024,4096]{1,0:T(8,128)(2,1)S(1)}, bf16[1024,4096]{1,0:T(8,128)(2,1)}, u32[]{:S(2)}) copy-start(bf16[1024,4096]{1,0:T(8,128)(2,1)} %copy-done) | copy-start | bytes 25165828
  153.3 12.3 %copy-start.8 = (f32[128]{0:T(128)S(1)}, f32[128]{0:T(128)}, u32[]{:S(2)}) copy-start(f32[128]{0:T(128)} %param.11) | copy-start | bytes 1540
  159.4 23.3 %all-to-all-start.3 = ((bf16[64,8,1152]{2,1,0:T(8,128)(2,1)}), bf16[64,8,1152]{2,1,0:T(8,128)(2,1)S(1)}, u32[]{:S(2)}, u32[]{:S(2)}) async-start(bf16[64,8,1152]{2,1,0:T(8,128)(2,1)} %bitcast.50), calls=%async_computation.3 | async-start | bytes 2359296 | tf_op jit(solution)/shard_map/all_to_all | solution.py:232

commit v3 on v2

--- a/solution.py
+++ b/solution.py
@@ -196,9 +196,8 @@
     gathered_parts = [
         gathered(slice(at, at + 32 * n)) for at, n in zip(starts_at, PARTS)
     ]
-    seen = shift(gathered_parts[0][0][0, :16], "c", 1)
-    swap_lo = shift(after(jnp.where(keeper, w_lo, below), seen), "c", 1)
-    swap_hi = shift(after(jnp.where(keeper, w_hi, above), seen), "c", 1)
+    swap_lo = shift(jnp.where(keeper, w_lo, below), "c", 1)
+    swap_hi = shift(jnp.where(keeper, w_hi, above), "c", 1)
     w_all = jnp.concatenate(
         [
             jnp.where(keeper, w_lo, swap_lo),
@@ -209,7 +208,7 @@
         axis=0,
     )
 
-    from_pair = after(jnp.where(low, p1[1024:], p3[1024:]), seen)
+    from_pair = jnp.where(low, p1[1024:], p3[1024:])
     from_pair = pick(from_pair, shift(from_pair, "c", 1))
     proj = (terms + from_pair.astype(jnp.float32)).astype(jnp.bfloat16)
     proj = jnp.concatenate([proj, proj], axis=0)

time: 186 us -> 184 us (0.989)
  waiting for transfers between devices: 71 us -> 77.7 us
  starting transfers between devices: 59.5 us -> 55.7 us
  other arithmetic: 24.7 us -> 21.1 us
    ppermute x23 -> x22, waiting for transfers between devices: 40.4 us -> 46.9 us  [move(): return lax.ppermute(value, axes if len(axes) > 1 else axes[0], pairs)]
    select_n x5 -> x2, other arithmetic: 6.8 us -> 1.61 us  [after(): return jnp.where(ready, value, jnp.zeros_like(value))]
    ppermute x23 -> x22, starting transfers between devices: 29.3 us -> 25.4 us  [move(): return lax.ppermute(value, axes if len(axes) > 1 else axes[0], pairs)]
    select_n x0 -> x3, other arithmetic: none -> 2.97 us  [the longest x1 1.82 us: on_device(): swap_lo = shift(jnp.where(keeper, w_lo, below), 'c', 1)]
    unnamed x23 -> x25, local copies, waits for them, and re-layouts: 6.44 us -> 6.45 us
  transfers between devices with their start and end apart: 27 -> 26, of which waited for: 11 -> 11; matrix products, arithmetic and copies ran while one was open for 13% -> 11% of each run, Pallas kernels for 9% -> 9%
where the time goes in v3:
time: 184 us; the launch traced here: 183 us
  waiting for transfers between devices  77.7 us (42%)
  starting transfers between devices  55.7 us (30%)
  other arithmetic  21.1 us (11%)
  Pallas kernels  15.8 us (9%)
  local copies, waits for them, and re-layouts  7.72 us (4%)
  between operations  4.48 us (2%)
    ppermute x22, waiting for transfers between devices, move(): return lax.ppermute(value, axes if len(axes) > 1 else axes[0], pairs)  46.9 us
    ppermute x22, starting transfers between devices, move(): return lax.ppermute(value, axes if len(axes) > 1 else axes[0], pairs)  25.4 us
    all_to_all x2, waiting for transfers between devices, finish(): lax.all_to_all(out.reshape(64, n, MESSAGE), PEERS, split_axis=0, concat_a...  19.5 us
    all_to_all x2, starting transfers between devices, finish(): lax.all_to_all(out.reshape(64, n, MESSAGE), PEERS, split_axis=0, concat_a...  19.2 us
    pallas_call x2, Pallas kernels, finish_part(): pl.pallas_call(finish_kernel, out_shape=jax.ShapeDtypeStruct((2, count, M...  15.8 us
    all_to_all x1, starting transfers between devices, on_device(): lax.all_to_all(copies, ('xh', 'z'), split_axis=0, concat_axis=0)  7.77 us
    all_to_all x1, waiting for transfers between devices, on_device(): lax.all_to_all(copies, ('xh', 'z'), split_axis=0, concat_axis=0)  7.72 us
    unnamed x25, local copies, waits for them, and re-layouts  6.45 us
  transfers between devices with their start and end apart: 26, of which 11 were waited for; matrix products, arithmetic and copies ran while one was open for 11% of the time, Pallas kernels for 9%

profile of v3, /device:TPU:0, one launch (start us, length us, event | category | flops | bytes accessed | tf_op | source)
XLA Modules:
  0.0 182.7 jit_solution(12935861798060292583)
XLA Ops:
  0.7 1.3 copy.12
  2.2 1.7 collective-permute-start
  3.9 2.9 %collective-permute-start.1 = (bf16[512,512]{1,0:T(8,128)(2,1)S(1)}, bf16[512,512]{1,0:T(8,128)(2,1)S(1)}, u32[]{:S(2)}, u32[]{:S(2)}) collective-permute-start(bf16[512,512]{1,0:T(8,128)(2,1)S(1)} %pad_maximum_fusion.6), channel_id=1, source_target_pairs={{0,16},{8,24},{16,0},{24,8},{1,17},{9,25},{17,1},{25,9},{2,18},{10... | collective-permute-start | bytes 1572872 | tf_op jit(solution)/shard_map/ppermute | solution.py:39
  6.8 1.3 collective-permute-start.2
  9.4 0.7 reshape.64
  10.1 7.8 %all-to-all-start = ((bf16[8,2,512]{2,1,0:T(2,128)(2,1)}), bf16[8,2,512]{2,1,0:T(2,128)(2,1)S(1)}, u32[]{:S(2)}, u32[]{:S(2)}) async-start(bf16[8,2,512]{2,1,0:T(2,128)(2,1)} %reshape.64), calls=%async_computation | async-start | bytes 32768 | tf_op jit(solution)/shard_map/all_to_all | solution.py:171
  17.8 7.7 %all-to-all-done = bf16[8,2,512]{2,1,0:T(2,128)(2,1)S(1)} async-done(((bf16[8,2,512]{2,1,0:T(2,128)(2,1)}), bf16[8,2,512]{2,1,0:T(2,128)(2,1)S(1)}, u32[]{:S(2)}, u32[]{:S(2)}) %all-to-all-start) | async-done | bytes 16416 | tf_op jit(solution)/shard_map/all_to_all | solution.py:171
  25.7 0.8 reshape.66
  26.5 3.3 %all-to-all-start.1 = ((bf16[4,2,4096]{2,1,0:T(2,128)(2,1)}), bf16[4,2,4096]{2,1,0:T(2,128)(2,1)S(1)}, u32[]{:S(2)}, u32[]{:S(2)}) async-start(bf16[4,2,4096]{2,1,0:T(2,128)(2,1)} %reshape.66), calls=%async_computation.1 | async-start | bytes 131072 | tf_op jit(solution)/shard_map/all_to_all | solution.py:173
  29.8 0.7 fusion.14
  31.8 3.5 %all-to-all-done.1 = bf16[4,2,4096]{2,1,0:T(2,128)(2,1)S(1)} async-done(((bf16[4,2,4096]{2,1,0:T(2,128)(2,1)}), bf16[4,2,4096]{2,1,0:T(2,128)(2,1)S(1)}, u32[]{:S(2)}, u32[]{:S(2)}) %all-to-all-start.1) | async-done | bytes 65568 | tf_op jit(solution)/shard_map/all_to_all | solution.py:173
  38.9 1.6 slice_select_fusion.1
  40.5 2.0 %collective-permute-start.12 = (bf16[256,4096]{1,0:T(8,128)(2,1)}, bf16[256,4096]{1,0:T(8,128)(2,1)}, u32[]{:S(2)}, u32[]{:S(2)}) collective-permute-start(bf16[256,4096]{1,0:T(8,128)(2,1)} %get-tuple-element.6), channel_id=1, source_target_pairs={{8,48},{24,32},{32,8},{48,24},{9,49},{25,33},{33,9},{49,25},{10,50... | collective-permute-start | bytes 6291464 | tf_op jit(solution)/shard_map/ppermute | solution.py:39
  42.6 1.1 pad_maximum_fusion.1
  44.0 1.7 collective-permute-start.7
  45.8 0.8 collective-permute-start.14
  46.6 1.1 fusion.7
  47.7 0.7 collective-permute-start.6
  48.4 11.1 %collective-permute-done.5 = bf16[1088,512]{1,0:T(8,128)(2,1)} collective-permute-done((bf16[1088,512]{1,0:T(8,128)(2,1)}, bf16[1088,512]{1,0:T(8,128)(2,1)}, u32[]{:S(2)}, u32[]{:S(2)}) %collective-permute-start.5) | collective-permute-done | bytes 1114144 | tf_op jit(solution)/shard_map/ppermute | solution.py:39
  59.5 13.5 %collective-permute-done.7 = bf16[1088,512]{1,0:T(8,128)(2,1)} collective-permute-done((bf16[1088,512]{1,0:T(8,128)(2,1)}, bf16[1088,512]{1,0:T(8,128)(2,1)}, u32[]{:S(2)}, u32[]{:S(2)}) %collective-permute-start.7) | collective-permute-done | bytes 1114144 | tf_op jit(solution)/shard_map/ppermute | solution.py:39
  72.9 0.9 slice_select_fusion.10
  74.0 1.3 slice_bitcast_fusion.8
  75.3 1.3 slice_bitcast_fusion.6
  76.5 1.8 broadcast_select_fusion.5
  80.2 1.2 pad_maximum_fusion.5
  81.5 1.7 collective-permute-start.17
  83.1 1.6 collective-permute-start.18
  84.9 2.4 %collective-permute-done.17 = bf16[128,256]{1,0:T(8,128)(2,1)S(1)} collective-permute-done((bf16[128,256]{1,0:T(8,128)(2,1)S(1)}, bf16[128,256]{1,0:T(8,128)(2,1)S(1)}, u32[]{:S(2)}, u32[]{:S(2)}) %collective-permute-start.17) | collective-permute-done | bytes 65568 | tf_op jit(solution)/shard_map/ppermute | solution.py:39
  87.3 2.5 %collective-permute-start.8 = (bf16[4,256,512]{2,1,0:T(8,128)(2,1)S(1)}, bf16[4,256,512]{2,1,0:T(8,128)(2,1)S(1)}, u32[]{:S(2)}, u32[]{:S(2)}) collective-permute-start(bf16[4,256,512]{2,1,0:T(8,128)(2,1)S(1)} %pad_maximum_fusion.3), channel_id=1, source_target_pairs={{0,3},{1,0},{2,1},{3,2},{4,7},{5,4},{6,5},{7,6},{32,100},{33,101},... | collective-permute-start | bytes 3145736 | tf_op jit(solution)/shard_map/ppermute | solution.py:39
  89.7 0.9 collective-permute-start.19
  90.7 1.2 collective-permute-start.21
  91.9 1.9 %broadcast_select_fusion.4 = (bf16[256,4096]{1,0:T(8,128)(2,1)S(1)}, bf16[256,4096]{1,0:T(8,128)(2,1)S(1)}) fusion(bf16[256,4096]{1,0:T(8,128)(2,1)} %get-tuple-element.6, bf16[256,4096]{1,0:T(8,128)(2,1)S(1)} %collective-permute-done.13, pred[]{:T(512)S(6)} %eq.73, bf16[256,4096]{1,0:T(8,128)(2,1)} %collective-permute-done.12), kind=kLoop, calls=%fused_computation.9 | loop fusion | flops 2097152 | bytes 10485761 | tf_op jit(solution)/shard_map/jit(_where)/select_n | solution.py:203
  93.8 1.3 collective-permute-start.9
  95.6 1.0 pad_maximum_fusion.w_all
  96.7 2.5 %collective-permute-start.20 = (bf16[4,256,512]{2,1,0:T(8,128)(2,1)S(1)}, bf16[4,256,512]{2,1,0:T(8,128)(2,1)}, u32[]{:S(2)}, u32[]{:S(2)}) collective-permute-start(bf16[4,256,512]{2,1,0:T(8,128)(2,1)S(1)} %pad_maximum_fusion.4.g0), channel_id=1, source_target_pairs={{0,2},{1,3},{2,0},{3,1},{4,6},{5,7},{6,4},{7,5},{32,36},{33,37},{3... | collective-permute-start | bytes 3145736 | tf_op jit(solution)/shard_map/ppermute | solution.py:39
  99.2 2.8 %collective-permute-done.8.g1 = bf16[4,256,512]{2,1,0:T(8,128)(2,1)S(1)} collective-permute-done((bf16[4,256,512]{2,1,0:T(8,128)(2,1)S(1)}, bf16[4,256,512]{2,1,0:T(8,128)(2,1)S(1)}, u32[]{:S(2)}, u32[]{:S(2)}) %collective-permute-start.8) | collective-permute-done | bytes 1048608 | tf_op jit(solution)/shard_map/ppermute | solution.py:39
  102.1 16.3 %collective-permute-done.9.g2 = bf16[4,256,512]{2,1,0:T(8,128)(2,1)S(1)} collective-permute-done((bf16[4,256,512]{2,1,0:T(8,128)(2,1)S(1)}, bf16[4,256,512]{2,1,0:T(8,128)(2,1)S(1)}, u32[]{:S(2)}, u32[]{:S(2)}) %collective-permute-start.9) | collective-permute-done | bytes 1048608 | tf_op jit(solution)/shard_map/ppermute | solution.py:39
  118.4 7.4 %shard_map.86 = bf16[2,256,1152]{2,1,0:T(8,128)(2,1)} custom-call(s32[19]{0:T(128)S(1)} %stack.139.table, bf16[4,256,512]{2,1,0:T(8,128)(2,1)S(1)} %pad_maximum_fusion.2.g0, bf16[4,256,512]{2,1,0:T(8,128)(2,1)S(1)} %collective-permute-done.8.g1, bf16[4,256,512]{2,1,0:T(8,128)(2,1)S(1)} %collective-permute-done.9.g2, ...), custom_call_target="tpu_custom_call" | custom-call | flops 4294967296 | bytes 14680064 | tf_op jit(solution)/shard_map/pallas_call | solution.py:126
  125.8 13.6 %all-to-all-start.2 = ((bf16[64,8,1152]{2,1,0:T(8,128)(2,1)}), bf16[64,8,1152]{2,1,0:T(8,128)(2,1)}, u32[]{:S(2)}, u32[]{:S(2)}) async-start(bf16[64,8,1152]{2,1,0:T(8,128)(2,1)} %bitcast.36), calls=%async_computation.2 | async-start | bytes 2359296 | tf_op jit(solution)/shard_map/all_to_all | solution.py:231
  139.4 3.4 %copy-done.1 = bf16[1024,4096]{1,0:T(8,128)(2,1)S(1)} copy-done((bf16[1024,4096]{1,0:T(8,128)(2,1)S(1)}, bf16[1024,4096]{1,0:T(8,128)(2,1)}, u32[]{:S(2)}) %copy-start.1) | copy-done | bytes 8388632
  142.8 8.4 %shard_map.87 = bf16[2,256,1152]{2,1,0:T(8,128)(2,1)} custom-call(s32[19]{0:T(128)S(1)} %stack.139.table, bf16[4,256,512]{2,1,0:T(8,128)(2,1)S(1)} %pad_maximum_fusion.4.g0, bf16[4,256,512]{2,1,0:T(8,128)(2,1)S(1)} %collective-permute-done.19.g1, bf16[4,256,512]{2,1,0:T(8,128)(2,1)} %collective-permute-done.20.g2, ...), custom_call_target="tpu_custom_call" | custom-call | flops 4294967296 | bytes 14680064 | tf_op jit(solution)/shard_map/pallas_call | solution.py:126
  151.2 6.2 %all-to-all-done.2 = bf16[64,8,1152]{2,1,0:T(8,128)(2,1)} async-done(((bf16[64,8,1152]{2,1,0:T(8,128)(2,1)}), bf16[64,8,1152]{2,1,0:T(8,128)(2,1)}, u32[]{:S(2)}, u32[]{:S(2)}) %all-to-all-start.2) | async-done | bytes 1179680 | tf_op jit(solution)/shard_map/all_to_all | solution.py:231
  157.4 5.6 %all-to-all-start.3 = ((bf16[64,8,1152]{2,1,0:T(8,128)(2,1)}), bf16[64,8,1152]{2,1,0:T(8,128)(2,1)S(1)}, u32[]{:S(2)}, u32[]{:S(2)}) async-start(bf16[64,8,1152]{2,1,0:T(8,128)(2,1)} %bitcast.48), calls=%async_computation.3 | async-start | bytes 2359296 | tf_op jit(solution)/shard_map/all_to_all | solution.py:231
  164.3 1.4 dynamic-slice_subtract_fusion
  165.7 1.6 convert_reduce_fusion.1
  167.3 13.3 %all-to-all-done.3 = bf16[64,8,1152]{2,1,0:T(8,128)(2,1)S(1)} async-done(((bf16[64,8,1152]{2,1,0:T(8,128)(2,1)}), bf16[64,8,1152]{2,1,0:T(8,128)(2,1)S(1)}, u32[]{:S(2)}, u32[]{:S(2)}) %all-to-all-start.3) | async-done | bytes 1179680 | tf_op jit(solution)/shard_map/all_to_all | solution.py:231
  181.2 0.8 pad_maximum_fusion.7
  182.0 0.7 fusion.13
  (77 shorter events, 7.9 us)
Async XLA Ops:
  0.6 34.9 %copy-start.6 = (bf16[512,512]{1,0:T(8,128)(2,1)S(1)}, bf16[512,512]{1,0:T(8,128)(2,1)}, u32[]{:S(2)}) copy-start(bf16[512,512]{1,0:T(8,128)(2,1)} %param.7) | copy-start | bytes 1572868
  0.6 8.7 %copy-start.7 = (bf16[16,64]{1,0:T(8,128)(2,1)S(1)}, bf16[16,64]{1,0:T(8,128)(2,1)}, u32[]{:S(2)}) copy-start(bf16[16,64]{1,0:T(8,128)(2,1)} %param.10) | copy-start | bytes 6148
  0.6 29.1 %copy-start.8 = (s32[4]{0:T(128)S(1)}, s32[4]{0:T(128)}, u32[]{:S(2)}) copy-start(s32[4]{0:T(128)} %param.9) | copy-start | bytes 52
  2.0 6.2 %collective-permute-start.3 = (bf16[16,512]{1,0:T(8,128)(2,1)S(1)}, bf16[16,512]{1,0:T(8,128)(2,1)S(1)}, u32[]{:S(2)}, u32[]{:S(2)}) collective-permute-start(bf16[16,512]{1,0:T(8,128)(2,1)S(1)} %slice_bitcast_fusion.10), channel_id=1, source_target_pairs={{0,32},{32,0},{1,33},{33,1},{2,34},{34,2},{3,35},{35,3},{4,36},{36... | collective-permute-start | bytes 49160 | tf_op jit(solution)/shard_map/ppermute | solution.py:39
  2.2 33.7 %collective-permute-start = (bf16[512,512]{1,0:T(8,128)(2,1)S(1)}, bf16[512,512]{1,0:T(8,128)(2,1)S(1)}, u32[]{:S(2)}, u32[]{:S(2)}) collective-permute-start(bf16[512,512]{1,0:T(8,128)(2,1)S(1)} %pad_maximum_fusion.6), channel_id=1, source_target_pairs={{0,8},{8,16},{16,24},{24,0},{1,9},{9,17},{17,25},{25,1},{2,10},{10... | collective-permute-start | bytes 1572872 | tf_op jit(solution)/shard_map/ppermute | solution.py:39
  3.9 32.0 %collective-permute-start.1 = (bf16[512,512]{1,0:T(8,128)(2,1)S(1)}, bf16[512,512]{1,0:T(8,128)(2,1)S(1)}, u32[]{:S(2)}, u32[]{:S(2)}) collective-permute-start(bf16[512,512]{1,0:T(8,128)(2,1)S(1)} %pad_maximum_fusion.6), channel_id=1, source_target_pairs={{0,16},{8,24},{16,0},{24,8},{1,17},{9,25},{17,1},{25,9},{2,18},{10... | collective-permute-start | bytes 1572872 | tf_op jit(solution)/shard_map/ppermute | solution.py:39
  6.8 29.1 %collective-permute-start.2 = (bf16[512,512]{1,0:T(8,128)(2,1)S(1)}, bf16[512,512]{1,0:T(8,128)(2,1)S(1)}, u32[]{:S(2)}, u32[]{:S(2)}) collective-permute-start(bf16[512,512]{1,0:T(8,128)(2,1)S(1)} %pad_maximum_fusion.6), channel_id=1, source_target_pairs={{0,24},{8,0},{16,8},{24,16},{1,25},{9,1},{17,9},{25,17},{2,26},{10... | collective-permute-start | bytes 1572872 | tf_op jit(solution)/shard_map/ppermute | solution.py:39
  10.1 15.5 %all-to-all-start = ((bf16[8,2,512]{2,1,0:T(2,128)(2,1)}), bf16[8,2,512]{2,1,0:T(2,128)(2,1)S(1)}, u32[]{:S(2)}, u32[]{:S(2)}) async-start(bf16[8,2,512]{2,1,0:T(2,128)(2,1)} %reshape.64), calls=%async_computation | async-start | bytes 32768 | tf_op jit(solution)/shard_map/all_to_all | solution.py:171
  26.5 8.9 %all-to-all-start.1 = ((bf16[4,2,4096]{2,1,0:T(2,128)(2,1)}), bf16[4,2,4096]{2,1,0:T(2,128)(2,1)S(1)}, u32[]{:S(2)}, u32[]{:S(2)}) async-start(bf16[4,2,4096]{2,1,0:T(2,128)(2,1)} %reshape.66), calls=%async_computation.1 | async-start | bytes 131072 | tf_op jit(solution)/shard_map/all_to_all | solution.py:173
  35.5 3.4 %copy-start.5 = (bf16[512,4096]{1,0:T(8,128)(2,1)S(1)}, bf16[512,4096]{1,0:T(8,128)(2,1)}, u32[]{:S(2)}) copy-start(bf16[512,4096]{1,0:T(8,128)(2,1)} %param.8) | copy-start | bytes 12582916
  35.8 1.4 collective-permute-start.4
  36.3 6.3 %copy-start.4 = (bf16[512,512]{1,0:T(8,128)(2,1)}, bf16[512,512]{1,0:T(8,128)(2,1)S(1)}, u32[]{:S(2)}) copy-start(bf16[512,512]{1,0:T(8,128)(2,1)S(1)} %get-tuple-element.13) | copy-start | bytes 1572868
  36.3 1.4 collective-permute-start.11
  40.5 38.4 %copy-start.2 = (bf16[256,4096]{1,0:T(8,128)(2,1)}, bf16[256,4096]{1,0:T(8,128)(2,1)S(1)}, u32[]{:S(2)}) copy-start(bf16[256,4096]{1,0:T(8,128)(2,1)S(1)} %get-tuple-element.7) | copy-start | bytes 6291460
  40.5 36.0 %collective-permute-start.12 = (bf16[256,4096]{1,0:T(8,128)(2,1)}, bf16[256,4096]{1,0:T(8,128)(2,1)}, u32[]{:S(2)}, u32[]{:S(2)}) collective-permute-start(bf16[256,4096]{1,0:T(8,128)(2,1)} %get-tuple-element.6), channel_id=1, source_target_pairs={{8,48},{24,32},{32,8},{48,24},{9,49},{25,33},{33,9},{49,25},{10,50... | collective-permute-start | bytes 6291464 | tf_op jit(solution)/shard_map/ppermute | solution.py:39
  43.6 15.8 %collective-permute-start.5 = (bf16[1088,512]{1,0:T(8,128)(2,1)}, bf16[1088,512]{1,0:T(8,128)(2,1)}, u32[]{:S(2)}, u32[]{:S(2)}) collective-permute-start(bf16[1088,512]{1,0:T(8,128)(2,1)} %pad_maximum_fusion.1), channel_id=1, source_target_pairs={{0,68},{1,69},{2,70},{3,71},{4,64},{5,65},{6,66},{7,67},{32,35},{3... | collective-permute-start | bytes 3342344 | tf_op jit(solution)/shard_map/ppermute | solution.py:39
  44.0 29.0 %collective-permute-start.7 = (bf16[1088,512]{1,0:T(8,128)(2,1)}, bf16[1088,512]{1,0:T(8,128)(2,1)}, u32[]{:S(2)}, u32[]{:S(2)}) collective-permute-start(bf16[1088,512]{1,0:T(8,128)(2,1)} %pad_maximum_fusion.1), channel_id=1, source_target_pairs={{0,64},{1,65},{2,66},{3,67},{4,68},{5,69},{6,70},{7,71},{32,33},{3... | collective-permute-start | bytes 3342344 | tf_op jit(solution)/shard_map/ppermute | solution.py:39
  45.8 33.2 %collective-permute-start.14 = (bf16[256,4096]{1,0:T(8,128)(2,1)S(1)}, bf16[256,4096]{1,0:T(8,128)(2,1)S(1)}, u32[]{:S(2)}, u32[]{:S(2)}) collective-permute-start(bf16[256,4096]{1,0:T(8,128)(2,1)S(1)} %get-tuple-element.7), channel_id=1, source_target_pairs={{8,32},{24,48},{32,24},{48,8},{9,33},{25,49},{33,25},{49,9},{10,34... | collective-permute-start | bytes 6291464 | tf_op jit(solution)/shard_map/ppermute | solution.py:39
  47.7 31.2 %collective-permute-start.6 = (bf16[1088,512]{1,0:T(8,128)(2,1)}, bf16[1088,512]{1,0:T(8,128)(2,1)S(1)}, u32[]{:S(2)}, u32[]{:S(2)}) collective-permute-start(bf16[1088,512]{1,0:T(8,128)(2,1)} %pad_maximum_fusion.1), channel_id=1, source_target_pairs={{0,4},{1,5},{2,6},{3,7},{4,0},{5,1},{6,2},{7,3},{32,34},{33,35},{3... | collective-permute-start | bytes 3342344 | tf_op jit(solution)/shard_map/ppermute | solution.py:39
  73.8 7.6 %collective-permute-start.16 = (bf16[64,512]{1,0:T(8,128)(2,1)S(1)}, bf16[64,512]{1,0:T(8,128)(2,1)S(1)}, u32[]{:S(2)}, u32[]{:S(2)}) collective-permute-start(bf16[64,512]{1,0:T(8,128)(2,1)S(1)} %slice_select_fusion.10), channel_id=1, source_target_pairs={{0,32},{32,0},{1,33},{33,1},{2,34},{34,2},{3,35},{35,3},{4,36},{36... | collective-permute-start | bytes 196616 | tf_op jit(solution)/shard_map/ppermute | solution.py:39
  78.4 12.3 %collective-permute-start.13 = (bf16[256,4096]{1,0:T(8,128)(2,1)S(1)}, bf16[256,4096]{1,0:T(8,128)(2,1)S(1)}, u32[]{:S(2)}, u32[]{:S(2)}) collective-permute-start(bf16[256,4096]{1,0:T(8,128)(2,1)S(1)} %broadcast_select_fusion.5), channel_id=1, source_target_pairs={{0,32},{32,0},{1,33},{33,1},{2,34},{34,2},{3,35},{35,3},{4,36},{36... | collective-permute-start | bytes 6291464 | tf_op jit(solution)/shard_map/ppermute | solution.py:39
  79.2 14.6 %collective-permute-start.15 = (bf16[256,4096]{1,0:T(8,128)(2,1)S(1)}, bf16[256,4096]{1,0:T(8,128)(2,1)S(1)}, u32[]{:S(2)}, u32[]{:S(2)}) collective-permute-start(bf16[256,4096]{1,0:T(8,128)(2,1)S(1)} %broadcast_select_fusion.3), channel_id=1, source_target_pairs={{0,32},{32,0},{1,33},{33,1},{2,34},{34,2},{3,35},{35,3},{4,36},{36... | collective-permute-start | bytes 6291464 | tf_op jit(solution)/shard_map/ppermute | solution.py:39
  79.5 17.2 %collective-permute-start.10 = (bf16[4,256,512]{2,1,0:T(8,128)(2,1)S(1)}, bf16[4,256,512]{2,1,0:T(8,128)(2,1)S(1)}, u32[]{:S(2)}, u32[]{:S(2)}) collective-permute-start(bf16[4,256,512]{2,1,0:T(8,128)(2,1)S(1)} %pad_maximum_fusion.3), channel_id=1, source_target_pairs={{0,1},{1,2},{2,3},{3,0},{4,5},{5,6},{6,7},{7,4},{32,96},{33,97},{3... | collective-permute-start | bytes 3145736 | tf_op jit(solution)/shard_map/ppermute | solution.py:39
  81.5 5.8 %collective-permute-start.17 = (bf16[128,256]{1,0:T(8,128)(2,1)S(1)}, bf16[128,256]{1,0:T(8,128)(2,1)S(1)}, u32[]{:S(2)}, u32[]{:S(2)}) collective-permute-start(bf16[128,256]{1,0:T(8,128)(2,1)S(1)} %get-tuple-element.40), channel_id=1, source_target_pairs={{0,8},{8,16},{16,24},{24,0},{1,9},{9,17},{17,25},{25,1},{2,10},{10... | collective-permute-start | bytes 196616 | tf_op jit(solution)/shard_map/ppermute | solution.py:39
  83.1 6.6 %collective-permute-start.18 = (bf16[128,256]{1,0:T(8,128)(2,1)S(1)}, bf16[128,256]{1,0:T(8,128)(2,1)S(1)}, u32[]{:S(2)}, u32[]{:S(2)}) collective-permute-start(bf16[128,256]{1,0:T(8,128)(2,1)S(1)} %get-tuple-element.41), channel_id=1, source_target_pairs={{0,24},{8,0},{16,8},{24,16},{1,25},{9,1},{17,9},{25,17},{2,26},{10... | collective-permute-start | bytes 196616 | tf_op jit(solution)/shard_map/ppermute | solution.py:39
  87.3 14.8 %collective-permute-start.8 = (bf16[4,256,512]{2,1,0:T(8,128)(2,1)S(1)}, bf16[4,256,512]{2,1,0:T(8,128)(2,1)S(1)}, u32[]{:S(2)}, u32[]{:S(2)}) collective-permute-start(bf16[4,256,512]{2,1,0:T(8,128)(2,1)S(1)} %pad_maximum_fusion.3), channel_id=1, source_target_pairs={{0,3},{1,0},{2,1},{3,2},{4,7},{5,4},{6,5},{7,6},{32,100},{33,101},... | collective-permute-start | bytes 3145736 | tf_op jit(solution)/shard_map/ppermute | solution.py:39
  89.7 49.6 %collective-permute-start.19 = (bf16[4,256,512]{2,1,0:T(8,128)(2,1)}, bf16[4,256,512]{2,1,0:T(8,128)(2,1)S(1)}, u32[]{:S(2)}, u32[]{:S(2)}) collective-permute-start(bf16[4,256,512]{2,1,0:T(8,128)(2,1)} %pad_maximum_fusion.5), channel_id=1, source_target_pairs={{0,3},{1,0},{2,1},{3,2},{4,7},{5,4},{6,5},{7,6},{32,100},{33,101},... | collective-permute-start | bytes 3145736 | tf_op jit(solution)/shard_map/ppermute | solution.py:39
  90.7 4.5 %copy-start.3 = (bf16[256,4096]{1,0:T(8,128)(2,1)S(1)}, bf16[256,4096]{1,0:T(8,128)(2,1)}, u32[]{:S(2)}) copy-start(bf16[256,4096]{1,0:T(8,128)(2,1)} %copy-done.2) | copy-start | bytes 6291460
  90.7 48.7 %collective-permute-start.21 = (bf16[4,256,512]{2,1,0:T(8,128)(2,1)}, bf16[4,256,512]{2,1,0:T(8,128)(2,1)}, u32[]{:S(2)}, u32[]{:S(2)}) collective-permute-start(bf16[4,256,512]{2,1,0:T(8,128)(2,1)} %pad_maximum_fusion.5), channel_id=1, source_target_pairs={{0,1},{1,2},{2,3},{3,0},{4,5},{5,6},{6,7},{7,4},{32,96},{33,97},{3... | collective-permute-start | bytes 3145736 | tf_op jit(solution)/shard_map/ppermute | solution.py:39
  93.8 24.6 %collective-permute-start.9 = (bf16[4,256,512]{2,1,0:T(8,128)(2,1)S(1)}, bf16[4,256,512]{2,1,0:T(8,128)(2,1)S(1)}, u32[]{:S(2)}, u32[]{:S(2)}) collective-permute-start(bf16[4,256,512]{2,1,0:T(8,128)(2,1)S(1)} %pad_maximum_fusion.2.g0), channel_id=1, source_target_pairs={{0,2},{1,3},{2,0},{3,1},{4,6},{5,7},{6,4},{7,5},{32,36},{33,37},{3... | collective-permute-start | bytes 3145736 | tf_op jit(solution)/shard_map/ppermute | solution.py:39
  96.7 29.1 %copy-start = (bf16[1024,4096]{1,0:T(8,128)(2,1)}, bf16[1024,4096]{1,0:T(8,128)(2,1)S(1)}, u32[]{:S(2)}) copy-start(bf16[1024,4096]{1,0:T(8,128)(2,1)S(1)} %pad_maximum_fusion.w_all) | copy-start | bytes 25165828
  96.7 42.7 %collective-permute-start.20 = (bf16[4,256,512]{2,1,0:T(8,128)(2,1)S(1)}, bf16[4,256,512]{2,1,0:T(8,128)(2,1)}, u32[]{:S(2)}, u32[]{:S(2)}) collective-permute-start(bf16[4,256,512]{2,1,0:T(8,128)(2,1)S(1)} %pad_maximum_fusion.4.g0), channel_id=1, source_target_pairs={{0,2},{1,3},{2,0},{3,1},{4,6},{5,7},{6,4},{7,5},{32,36},{33,37},{3... | collective-permute-start | bytes 3145736 | tf_op jit(solution)/shard_map/ppermute | solution.py:39
  125.8 31.6 %all-to-all-start.2 = ((bf16[64,8,1152]{2,1,0:T(8,128)(2,1)}), bf16[64,8,1152]{2,1,0:T(8,128)(2,1)}, u32[]{:S(2)}, u32[]{:S(2)}) async-start(bf16[64,8,1152]{2,1,0:T(8,128)(2,1)} %bitcast.36), calls=%async_computation.2 | async-start | bytes 2359296 | tf_op jit(solution)/shard_map/all_to_all | solution.py:231
  139.4 3.4 %copy-start.1 = (bf16[1024,4096]{1,0:T(8,128)(2,1)S(1)}, bf16[1024,4096]{1,0:T(8,128)(2,1)}, u32[]{:S(2)}) copy-start(bf16[1024,4096]{1,0:T(8,128)(2,1)} %copy-done) | copy-start | bytes 25165828
  151.2 12.5 %copy-start.9 = (f32[128]{0:T(128)S(1)}, f32[128]{0:T(128)}, u32[]{:S(2)}) copy-start(f32[128]{0:T(128)} %param.11) | copy-start | bytes 1540
  157.4 23.3 %all-to-all-start.3 = ((bf16[64,8,1152]{2,1,0:T(8,128)(2,1)}), bf16[64,8,1152]{2,1,0:T(8,128)(2,1)S(1)}, u32[]{:S(2)}, u32[]{:S(2)}) async-start(bf16[64,8,1152]{2,1,0:T(8,128)(2,1)} %bitcast.48), calls=%async_computation.3 | async-start | bytes 2359296 | tf_op jit(solution)/shard_map/all_to_all | solution.py:231

commit v4 on v3

--- a/solution.py
+++ b/solution.py
@@ -79,14 +79,14 @@
     first_core = table[16] == 1
 
     def on_block(block, coupled):
-        rows = pl.multiple_of(block * 256, 256)
+        rows = pl.multiple_of(block * 512, 512)
         sums = {}
         for g in range(4):
             for u in range(4):
                 column = pl.multiple_of(table[4 * g + u] * 512, 512)
                 term = lax.dot_general(
                     pieces[g][u],
-                    w_all[pl.ds(rows, 256), pl.ds(column, 512)],
+                    w_all[pl.ds(rows, 512), pl.ds(column, 512)],
                     (((1,), (1,)), ((), ())),
                     preferred_element_type=jnp.float32,
                 )
@@ -95,24 +95,24 @@
         mixed = (sums[0, 1], sums[1, 0])
         same = sums[0, 0] + jnp.where(first_core, mixed[1], mixed[0])
         opposite = sums[1, 1] + jnp.where(first_core, mixed[0], mixed[1])
-        own = jnp.where(block < 2, 2.0, 0.0)
-        same = own * bt[:, pl.ds(pl.multiple_of(lax.rem(rows, 512), 256), 256)].astype(jnp.float32) - same
+        own = jnp.where(block < 1, 2.0, 0.0)
+        same = own * bt[...].astype(jnp.float32) - same
         added = []
         for slot, part in enumerate((same, -opposite)):
             rounded = part.astype(jnp.bfloat16)
-            out[table[17 + slot], :, pl.ds(rows, 256)] = rounded
+            out[table[17 + slot], :, pl.ds(rows, 512)] = rounded
             added.append(
                 coupled[slot]
                 + lax.dot_general(
                     rounded,
-                    proj[:, pl.ds(rows, 256)],
+                    proj[:, pl.ds(rows, 512)],
                     (((1,), (1,)), ((), ())),
                     preferred_element_type=jnp.float32,
                 )
             )
         return tuple(added)
 
-    coupled = lax.fori_loop(0, 4, on_block, (jnp.zeros((count, 2 * NVEC), jnp.float32),) * 2)
+    coupled = lax.fori_loop(0, 2, on_block, (jnp.zeros((count, 2 * NVEC), jnp.float32),) * 2)
     high_lanes = lax.broadcasted_iota(jnp.int32, (count, 2 * NVEC), 1) < NVEC
     for slot in range(2):
         high = coupled[slot].astype(jnp.bfloat16).astype(jnp.float32)

time: 184 us -> 183 us (level)
  transfers between devices with their start and end apart: 26 -> 26, of which waited for: 11 -> 11; matrix products, arithmetic and copies ran while one was open for 11% -> 11% of each run, Pallas kernels for 9% -> 8%
where the time goes in v4:
time: 183 us; the launch traced here: 182 us
  waiting for transfers between devices  78.4 us (43%)
  starting transfers between devices  55.7 us (30%)
  other arithmetic  21.1 us (12%)
  Pallas kernels  14.4 us (8%)
  local copies, waits for them, and re-layouts  7.72 us (4%)
  between operations  4.48 us (2%)
    ppermute x22, waiting for transfers between devices, move(): return lax.ppermute(value, axes if len(axes) > 1 else axes[0], pairs)  46.9 us
    ppermute x22, starting transfers between devices, move(): return lax.ppermute(value, axes if len(axes) > 1 else axes[0], pairs)  25.4 us
    all_to_all x2, waiting for transfers between devices, finish(): lax.all_to_all(out.reshape(64, n, MESSAGE), PEERS, split_axis=0, concat_a...  20.2 us
    all_to_all x2, starting transfers between devices, finish(): lax.all_to_all(out.reshape(64, n, MESSAGE), PEERS, split_axis=0, concat_a...  19.2 us
    pallas_call x2, Pallas kernels, finish_part(): pl.pallas_call(finish_kernel, out_shape=jax.ShapeDtypeStruct((2, count, M...  14.4 us
    all_to_all x1, starting transfers between devices, on_device(): lax.all_to_all(copies, ('xh', 'z'), split_axis=0, concat_axis=0)  7.77 us
    all_to_all x1, waiting for transfers between devices, on_device(): lax.all_to_all(copies, ('xh', 'z'), split_axis=0, concat_axis=0)  7.72 us
    unnamed x25, local copies, waits for them, and re-layouts  6.45 us
  transfers between devices with their start and end apart: 26, of which 11 were waited for; matrix products, arithmetic and copies ran while one was open for 11% of the time, Pallas kernels for 8%

profile of v4, /device:TPU:0, one launch (start us, length us, event | category | flops | bytes accessed | tf_op | source)
XLA Modules:
  0.0 182.0 jit_solution(12832839188376477535)
XLA Ops:
  0.7 1.3 copy.12
  2.2 1.7 collective-permute-start
  3.9 2.9 %collective-permute-start.1 = (bf16[512,512]{1,0:T(8,128)(2,1)S(1)}, bf16[512,512]{1,0:T(8,128)(2,1)S(1)}, u32[]{:S(2)}, u32[]{:S(2)}) collective-permute-start(bf16[512,512]{1,0:T(8,128)(2,1)S(1)} %pad_maximum_fusion.6), channel_id=1, source_target_pairs={{0,16},{8,24},{16,0},{24,8},{1,17},{9,25},{17,1},{25,9},{2,18},{10... | collective-permute-start | bytes 1572872 | tf_op jit(solution)/shard_map/ppermute | solution.py:39
  6.8 1.3 collective-permute-start.2
  9.4 0.7 reshape.64
  10.1 7.8 %all-to-all-start = ((bf16[8,2,512]{2,1,0:T(2,128)(2,1)}), bf16[8,2,512]{2,1,0:T(2,128)(2,1)S(1)}, u32[]{:S(2)}, u32[]{:S(2)}) async-start(bf16[8,2,512]{2,1,0:T(2,128)(2,1)} %reshape.64), calls=%async_computation | async-start | bytes 32768 | tf_op jit(solution)/shard_map/all_to_all | solution.py:171
  17.8 7.7 %all-to-all-done = bf16[8,2,512]{2,1,0:T(2,128)(2,1)S(1)} async-done(((bf16[8,2,512]{2,1,0:T(2,128)(2,1)}), bf16[8,2,512]{2,1,0:T(2,128)(2,1)S(1)}, u32[]{:S(2)}, u32[]{:S(2)}) %all-to-all-start) | async-done | bytes 16416 | tf_op jit(solution)/shard_map/all_to_all | solution.py:171
  25.7 0.8 reshape.66
  26.5 3.3 %all-to-all-start.1 = ((bf16[4,2,4096]{2,1,0:T(2,128)(2,1)}), bf16[4,2,4096]{2,1,0:T(2,128)(2,1)S(1)}, u32[]{:S(2)}, u32[]{:S(2)}) async-start(bf16[4,2,4096]{2,1,0:T(2,128)(2,1)} %reshape.66), calls=%async_computation.1 | async-start | bytes 131072 | tf_op jit(solution)/shard_map/all_to_all | solution.py:173
  29.8 0.7 fusion.14
  31.8 3.5 %all-to-all-done.1 = bf16[4,2,4096]{2,1,0:T(2,128)(2,1)S(1)} async-done(((bf16[4,2,4096]{2,1,0:T(2,128)(2,1)}), bf16[4,2,4096]{2,1,0:T(2,128)(2,1)S(1)}, u32[]{:S(2)}, u32[]{:S(2)}) %all-to-all-start.1) | async-done | bytes 65568 | tf_op jit(solution)/shard_map/all_to_all | solution.py:173
  38.9 1.6 slice_select_fusion.1
  40.5 2.0 %collective-permute-start.12 = (bf16[256,4096]{1,0:T(8,128)(2,1)}, bf16[256,4096]{1,0:T(8,128)(2,1)}, u32[]{:S(2)}, u32[]{:S(2)}) collective-permute-start(bf16[256,4096]{1,0:T(8,128)(2,1)} %get-tuple-element.6), channel_id=1, source_target_pairs={{8,48},{24,32},{32,8},{48,24},{9,49},{25,33},{33,9},{49,25},{10,50... | collective-permute-start | bytes 6291464 | tf_op jit(solution)/shard_map/ppermute | solution.py:39
  42.6 1.1 pad_maximum_fusion.1
  44.0 1.7 collective-permute-start.7
  45.8 0.8 collective-permute-start.14
  46.6 1.1 fusion.7
  47.7 0.7 collective-permute-start.6
  48.4 11.1 %collective-permute-done.5 = bf16[1088,512]{1,0:T(8,128)(2,1)} collective-permute-done((bf16[1088,512]{1,0:T(8,128)(2,1)}, bf16[1088,512]{1,0:T(8,128)(2,1)}, u32[]{:S(2)}, u32[]{:S(2)}) %collective-permute-start.5) | collective-permute-done | bytes 1114144 | tf_op jit(solution)/shard_map/ppermute | solution.py:39
  59.5 13.5 %collective-permute-done.7 = bf16[1088,512]{1,0:T(8,128)(2,1)} collective-permute-done((bf16[1088,512]{1,0:T(8,128)(2,1)}, bf16[1088,512]{1,0:T(8,128)(2,1)}, u32[]{:S(2)}, u32[]{:S(2)}) %collective-permute-start.7) | collective-permute-done | bytes 1114144 | tf_op jit(solution)/shard_map/ppermute | solution.py:39
  72.9 0.9 slice_select_fusion.10
  74.0 1.3 slice_bitcast_fusion.8
  75.3 1.3 slice_bitcast_fusion.6
  76.5 1.8 %broadcast_select_fusion.5 = bf16[256,4096]{1,0:T(8,128)(2,1)S(1)} fusion(bf16[256,4096]{1,0:T(8,128)(2,1)} %get-tuple-element.6, bf16[256,4096]{1,0:T(8,128)(2,1)} %collective-permute-done.12, pred[]{:T(512)S(6)} %eq.73), kind=kLoop, calls=%fused_computation.10 | loop fusion | flops 1048576 | bytes 6291457 | tf_op jit(solution)/shard_map/jit(_where)/select_n | solution.py:199
  80.2 1.2 pad_maximum_fusion.5
  81.5 1.7 collective-permute-start.17
  83.1 1.6 collective-permute-start.18
  84.9 2.4 %collective-permute-done.17 = bf16[128,256]{1,0:T(8,128)(2,1)S(1)} collective-permute-done((bf16[128,256]{1,0:T(8,128)(2,1)S(1)}, bf16[128,256]{1,0:T(8,128)(2,1)S(1)}, u32[]{:S(2)}, u32[]{:S(2)}) %collective-permute-start.17) | collective-permute-done | bytes 65568 | tf_op jit(solution)/shard_map/ppermute | solution.py:39
  87.3 2.5 %collective-permute-start.8 = (bf16[4,256,512]{2,1,0:T(8,128)(2,1)S(1)}, bf16[4,256,512]{2,1,0:T(8,128)(2,1)S(1)}, u32[]{:S(2)}, u32[]{:S(2)}) collective-permute-start(bf16[4,256,512]{2,1,0:T(8,128)(2,1)S(1)} %pad_maximum_fusion.3), channel_id=1, source_target_pairs={{0,3},{1,0},{2,1},{3,2},{4,7},{5,4},{6,5},{7,6},{32,100},{33,101},... | collective-permute-start | bytes 3145736 | tf_op jit(solution)/shard_map/ppermute | solution.py:39
  89.7 0.9 collective-permute-start.19
  90.7 1.2 collective-permute-start.21
  91.9 1.9 %broadcast_select_fusion.4 = (bf16[256,4096]{1,0:T(8,128)(2,1)S(1)}, bf16[256,4096]{1,0:T(8,128)(2,1)S(1)}) fusion(bf16[256,4096]{1,0:T(8,128)(2,1)} %get-tuple-element.6, bf16[256,4096]{1,0:T(8,128)(2,1)S(1)} %collective-permute-done.13, pred[]{:T(512)S(6)} %eq.73, bf16[256,4096]{1,0:T(8,128)(2,1)} %collective-permute-done.12), kind=kLoop, calls=%fused_computation.9 | loop fusion | flops 2097152 | bytes 10485761 | tf_op jit(solution)/shard_map/jit(_where)/select_n | solution.py:203
  93.8 1.3 collective-permute-start.9
  95.6 1.0 pad_maximum_fusion.w_all
  96.7 2.5 %collective-permute-start.20 = (bf16[4,256,512]{2,1,0:T(8,128)(2,1)S(1)}, bf16[4,256,512]{2,1,0:T(8,128)(2,1)}, u32[]{:S(2)}, u32[]{:S(2)}) collective-permute-start(bf16[4,256,512]{2,1,0:T(8,128)(2,1)S(1)} %pad_maximum_fusion.4.g0), channel_id=1, source_target_pairs={{0,2},{1,3},{2,0},{3,1},{4,6},{5,7},{6,4},{7,5},{32,36},{33,37},{3... | collective-permute-start | bytes 3145736 | tf_op jit(solution)/shard_map/ppermute | solution.py:39
  99.2 2.8 %collective-permute-done.8.g1 = bf16[4,256,512]{2,1,0:T(8,128)(2,1)S(1)} collective-permute-done((bf16[4,256,512]{2,1,0:T(8,128)(2,1)S(1)}, bf16[4,256,512]{2,1,0:T(8,128)(2,1)S(1)}, u32[]{:S(2)}, u32[]{:S(2)}) %collective-permute-start.8) | collective-permute-done | bytes 1048608 | tf_op jit(solution)/shard_map/ppermute | solution.py:39
  102.1 16.3 %collective-permute-done.9.g2 = bf16[4,256,512]{2,1,0:T(8,128)(2,1)S(1)} collective-permute-done((bf16[4,256,512]{2,1,0:T(8,128)(2,1)S(1)}, bf16[4,256,512]{2,1,0:T(8,128)(2,1)S(1)}, u32[]{:S(2)}, u32[]{:S(2)}) %collective-permute-start.9) | collective-permute-done | bytes 1048608 | tf_op jit(solution)/shard_map/ppermute | solution.py:39
  118.4 6.7 %shard_map.86 = bf16[2,256,1152]{2,1,0:T(8,128)(2,1)} custom-call(s32[19]{0:T(128)S(1)} %stack.139.table, bf16[4,256,512]{2,1,0:T(8,128)(2,1)S(1)} %pad_maximum_fusion.2.g0, bf16[4,256,512]{2,1,0:T(8,128)(2,1)S(1)} %collective-permute-done.8.g1, bf16[4,256,512]{2,1,0:T(8,128)(2,1)S(1)} %collective-permute-done.9.g2, ...), custom_call_target="tpu_custom_call" | custom-call | flops 4294967296 | bytes 14680064 | tf_op jit(solution)/shard_map/pallas_call | solution.py:126
  125.1 13.6 %all-to-all-start.2 = ((bf16[64,8,1152]{2,1,0:T(8,128)(2,1)}), bf16[64,8,1152]{2,1,0:T(8,128)(2,1)}, u32[]{:S(2)}, u32[]{:S(2)}) async-start(bf16[64,8,1152]{2,1,0:T(8,128)(2,1)} %bitcast.36), calls=%async_computation.2 | async-start | bytes 2359296 | tf_op jit(solution)/shard_map/all_to_all | solution.py:231
  138.8 3.4 %copy-done.1 = bf16[1024,4096]{1,0:T(8,128)(2,1)S(1)} copy-done((bf16[1024,4096]{1,0:T(8,128)(2,1)S(1)}, bf16[1024,4096]{1,0:T(8,128)(2,1)}, u32[]{:S(2)}) %copy-start.1) | copy-done | bytes 8388632
  142.1 7.7 %shard_map.87 = bf16[2,256,1152]{2,1,0:T(8,128)(2,1)} custom-call(s32[19]{0:T(128)S(1)} %stack.139.table, bf16[4,256,512]{2,1,0:T(8,128)(2,1)S(1)} %pad_maximum_fusion.4.g0, bf16[4,256,512]{2,1,0:T(8,128)(2,1)S(1)} %collective-permute-done.19.g1, bf16[4,256,512]{2,1,0:T(8,128)(2,1)} %collective-permute-done.20.g2, ...), custom_call_target="tpu_custom_call" | custom-call | flops 4294967296 | bytes 14680064 | tf_op jit(solution)/shard_map/pallas_call | solution.py:126
  149.8 6.8 %all-to-all-done.2 = bf16[64,8,1152]{2,1,0:T(8,128)(2,1)} async-done(((bf16[64,8,1152]{2,1,0:T(8,128)(2,1)}), bf16[64,8,1152]{2,1,0:T(8,128)(2,1)}, u32[]{:S(2)}, u32[]{:S(2)}) %all-to-all-start.2) | async-done | bytes 1179680 | tf_op jit(solution)/shard_map/all_to_all | solution.py:231
  156.7 5.6 %all-to-all-start.3 = ((bf16[64,8,1152]{2,1,0:T(8,128)(2,1)}), bf16[64,8,1152]{2,1,0:T(8,128)(2,1)S(1)}, u32[]{:S(2)}, u32[]{:S(2)}) async-start(bf16[64,8,1152]{2,1,0:T(8,128)(2,1)} %bitcast.48), calls=%async_computation.3 | async-start | bytes 2359296 | tf_op jit(solution)/shard_map/all_to_all | solution.py:231
  163.6 1.4 dynamic-slice_subtract_fusion
  165.0 1.6 convert_reduce_fusion.1
  166.6 13.3 %all-to-all-done.3 = bf16[64,8,1152]{2,1,0:T(8,128)(2,1)S(1)} async-done(((bf16[64,8,1152]{2,1,0:T(8,128)(2,1)}), bf16[64,8,1152]{2,1,0:T(8,128)(2,1)S(1)}, u32[]{:S(2)}, u32[]{:S(2)}) %all-to-all-start.3) | async-done | bytes 1179680 | tf_op jit(solution)/shard_map/all_to_all | solution.py:231
  180.5 0.8 pad_maximum_fusion.7
  181.3 0.7 fusion.13
  (77 shorter events, 7.9 us)
Async XLA Ops:
  0.6 34.9 %copy-start.6 = (bf16[512,512]{1,0:T(8,128)(2,1)S(1)}, bf16[512,512]{1,0:T(8,128)(2,1)}, u32[]{:S(2)}) copy-start(bf16[512,512]{1,0:T(8,128)(2,1)} %param.7) | copy-start | bytes 1572868
  0.6 8.7 %copy-start.7 = (bf16[16,64]{1,0:T(8,128)(2,1)S(1)}, bf16[16,64]{1,0:T(8,128)(2,1)}, u32[]{:S(2)}) copy-start(bf16[16,64]{1,0:T(8,128)(2,1)} %param.10) | copy-start | bytes 6148
  0.6 29.1 %copy-start.8 = (s32[4]{0:T(128)S(1)}, s32[4]{0:T(128)}, u32[]{:S(2)}) copy-start(s32[4]{0:T(128)} %param.9) | copy-start | bytes 52
  2.0 6.2 %collective-permute-start.3 = (bf16[16,512]{1,0:T(8,128)(2,1)S(1)}, bf16[16,512]{1,0:T(8,128)(2,1)S(1)}, u32[]{:S(2)}, u32[]{:S(2)}) collective-permute-start(bf16[16,512]{1,0:T(8,128)(2,1)S(1)} %slice_bitcast_fusion.10), channel_id=1, source_target_pairs={{0,32},{32,0},{1,33},{33,1},{2,34},{34,2},{3,35},{35,3},{4,36},{36... | collective-permute-start | bytes 49160 | tf_op jit(solution)/shard_map/ppermute | solution.py:39
  2.2 33.7 %collective-permute-start = (bf16[512,512]{1,0:T(8,128)(2,1)S(1)}, bf16[512,512]{1,0:T(8,128)(2,1)S(1)}, u32[]{:S(2)}, u32[]{:S(2)}) collective-permute-start(bf16[512,512]{1,0:T(8,128)(2,1)S(1)} %pad_maximum_fusion.6), channel_id=1, source_target_pairs={{0,8},{8,16},{16,24},{24,0},{1,9},{9,17},{17,25},{25,1},{2,10},{10... | collective-permute-start | bytes 1572872 | tf_op jit(solution)/shard_map/ppermute | solution.py:39
  3.9 32.0 %collective-permute-start.1 = (bf16[512,512]{1,0:T(8,128)(2,1)S(1)}, bf16[512,512]{1,0:T(8,128)(2,1)S(1)}, u32[]{:S(2)}, u32[]{:S(2)}) collective-permute-start(bf16[512,512]{1,0:T(8,128)(2,1)S(1)} %pad_maximum_fusion.6), channel_id=1, source_target_pairs={{0,16},{8,24},{16,0},{24,8},{1,17},{9,25},{17,1},{25,9},{2,18},{10... | collective-permute-start | bytes 1572872 | tf_op jit(solution)/shard_map/ppermute | solution.py:39
  6.8 29.1 %collective-permute-start.2 = (bf16[512,512]{1,0:T(8,128)(2,1)S(1)}, bf16[512,512]{1,0:T(8,128)(2,1)S(1)}, u32[]{:S(2)}, u32[]{:S(2)}) collective-permute-start(bf16[512,512]{1,0:T(8,128)(2,1)S(1)} %pad_maximum_fusion.6), channel_id=1, source_target_pairs={{0,24},{8,0},{16,8},{24,16},{1,25},{9,1},{17,9},{25,17},{2,26},{10... | collective-permute-start | bytes 1572872 | tf_op jit(solution)/shard_map/ppermute | solution.py:39
  10.1 15.5 %all-to-all-start = ((bf16[8,2,512]{2,1,0:T(2,128)(2,1)}), bf16[8,2,512]{2,1,0:T(2,128)(2,1)S(1)}, u32[]{:S(2)}, u32[]{:S(2)}) async-start(bf16[8,2,512]{2,1,0:T(2,128)(2,1)} %reshape.64), calls=%async_computation | async-start | bytes 32768 | tf_op jit(solution)/shard_map/all_to_all | solution.py:171
  26.5 8.9 %all-to-all-start.1 = ((bf16[4,2,4096]{2,1,0:T(2,128)(2,1)}), bf16[4,2,4096]{2,1,0:T(2,128)(2,1)S(1)}, u32[]{:S(2)}, u32[]{:S(2)}) async-start(bf16[4,2,4096]{2,1,0:T(2,128)(2,1)} %reshape.66), calls=%async_computation.1 | async-start | bytes 131072 | tf_op jit(solution)/shard_map/all_to_all | solution.py:173
  35.5 3.4 %copy-start.5 = (bf16[512,4096]{1,0:T(8,128)(2,1)S(1)}, bf16[512,4096]{1,0:T(8,128)(2,1)}, u32[]{:S(2)}) copy-start(bf16[512,4096]{1,0:T(8,128)(2,1)} %param.8) | copy-start | bytes 12582916
  35.8 1.4 collective-permute-start.4
  36.3 6.3 %copy-start.4 = (bf16[512,512]{1,0:T(8,128)(2,1)}, bf16[512,512]{1,0:T(8,128)(2,1)S(1)}, u32[]{:S(2)}) copy-start(bf16[512,512]{1,0:T(8,128)(2,1)S(1)} %get-tuple-element.13) | copy-start | bytes 1572868
  36.3 1.4 collective-permute-start.11
  40.5 38.4 %copy-start.2 = (bf16[256,4096]{1,0:T(8,128)(2,1)}, bf16[256,4096]{1,0:T(8,128)(2,1)S(1)}, u32[]{:S(2)}) copy-start(bf16[256,4096]{1,0:T(8,128)(2,1)S(1)} %get-tuple-element.7) | copy-start | bytes 6291460
  40.5 36.0 %collective-permute-start.12 = (bf16[256,4096]{1,0:T(8,128)(2,1)}, bf16[256,4096]{1,0:T(8,128)(2,1)}, u32[]{:S(2)}, u32[]{:S(2)}) collective-permute-start(bf16[256,4096]{1,0:T(8,128)(2,1)} %get-tuple-element.6), channel_id=1, source_target_pairs={{8,48},{24,32},{32,8},{48,24},{9,49},{25,33},{33,9},{49,25},{10,50... | collective-permute-start | bytes 6291464 | tf_op jit(solution)/shard_map/ppermute | solution.py:39
  43.6 15.8 %collective-permute-start.5 = (bf16[1088,512]{1,0:T(8,128)(2,1)}, bf16[1088,512]{1,0:T(8,128)(2,1)}, u32[]{:S(2)}, u32[]{:S(2)}) collective-permute-start(bf16[1088,512]{1,0:T(8,128)(2,1)} %pad_maximum_fusion.1), channel_id=1, source_target_pairs={{0,68},{1,69},{2,70},{3,71},{4,64},{5,65},{6,66},{7,67},{32,35},{3... | collective-permute-start | bytes 3342344 | tf_op jit(solution)/shard_map/ppermute | solution.py:39
  44.0 29.0 %collective-permute-start.7 = (bf16[1088,512]{1,0:T(8,128)(2,1)}, bf16[1088,512]{1,0:T(8,128)(2,1)}, u32[]{:S(2)}, u32[]{:S(2)}) collective-permute-start(bf16[1088,512]{1,0:T(8,128)(2,1)} %pad_maximum_fusion.1), channel_id=1, source_target_pairs={{0,64},{1,65},{2,66},{3,67},{4,68},{5,69},{6,70},{7,71},{32,33},{3... | collective-permute-start | bytes 3342344 | tf_op jit(solution)/shard_map/ppermute | solution.py:39
  45.8 33.2 %collective-permute-start.14 = (bf16[256,4096]{1,0:T(8,128)(2,1)S(1)}, bf16[256,4096]{1,0:T(8,128)(2,1)S(1)}, u32[]{:S(2)}, u32[]{:S(2)}) collective-permute-start(bf16[256,4096]{1,0:T(8,128)(2,1)S(1)} %get-tuple-element.7), channel_id=1, source_target_pairs={{8,32},{24,48},{32,24},{48,8},{9,33},{25,49},{33,25},{49,9},{10,34... | collective-permute-start | bytes 6291464 | tf_op jit(solution)/shard_map/ppermute | solution.py:39
  47.7 31.2 %collective-permute-start.6 = (bf16[1088,512]{1,0:T(8,128)(2,1)}, bf16[1088,512]{1,0:T(8,128)(2,1)S(1)}, u32[]{:S(2)}, u32[]{:S(2)}) collective-permute-start(bf16[1088,512]{1,0:T(8,128)(2,1)} %pad_maximum_fusion.1), channel_id=1, source_target_pairs={{0,4},{1,5},{2,6},{3,7},{4,0},{5,1},{6,2},{7,3},{32,34},{33,35},{3... | collective-permute-start | bytes 3342344 | tf_op jit(solution)/shard_map/ppermute | solution.py:39
  73.8 7.6 %collective-permute-start.16 = (bf16[64,512]{1,0:T(8,128)(2,1)S(1)}, bf16[64,512]{1,0:T(8,128)(2,1)S(1)}, u32[]{:S(2)}, u32[]{:S(2)}) collective-permute-start(bf16[64,512]{1,0:T(8,128)(2,1)S(1)} %slice_select_fusion.10), channel_id=1, source_target_pairs={{0,32},{32,0},{1,33},{33,1},{2,34},{34,2},{3,35},{35,3},{4,36},{36... | collective-permute-start | bytes 196616 | tf_op jit(solution)/shard_map/ppermute | solution.py:39
  78.4 12.3 %collective-permute-start.13 = (bf16[256,4096]{1,0:T(8,128)(2,1)S(1)}, bf16[256,4096]{1,0:T(8,128)(2,1)S(1)}, u32[]{:S(2)}, u32[]{:S(2)}) collective-permute-start(bf16[256,4096]{1,0:T(8,128)(2,1)S(1)} %broadcast_select_fusion.5), channel_id=1, source_target_pairs={{0,32},{32,0},{1,33},{33,1},{2,34},{34,2},{3,35},{35,3},{4,36},{36... | collective-permute-start | bytes 6291464 | tf_op jit(solution)/shard_map/ppermute | solution.py:39
  79.2 14.6 %collective-permute-start.15 = (bf16[256,4096]{1,0:T(8,128)(2,1)S(1)}, bf16[256,4096]{1,0:T(8,128)(2,1)S(1)}, u32[]{:S(2)}, u32[]{:S(2)}) collective-permute-start(bf16[256,4096]{1,0:T(8,128)(2,1)S(1)} %broadcast_select_fusion.3), channel_id=1, source_target_pairs={{0,32},{32,0},{1,33},{33,1},{2,34},{34,2},{3,35},{35,3},{4,36},{36... | collective-permute-start | bytes 6291464 | tf_op jit(solution)/shard_map/ppermute | solution.py:39
  79.5 17.2 %collective-permute-start.10 = (bf16[4,256,512]{2,1,0:T(8,128)(2,1)S(1)}, bf16[4,256,512]{2,1,0:T(8,128)(2,1)S(1)}, u32[]{:S(2)}, u32[]{:S(2)}) collective-permute-start(bf16[4,256,512]{2,1,0:T(8,128)(2,1)S(1)} %pad_maximum_fusion.3), channel_id=1, source_target_pairs={{0,1},{1,2},{2,3},{3,0},{4,5},{5,6},{6,7},{7,4},{32,96},{33,97},{3... | collective-permute-start | bytes 3145736 | tf_op jit(solution)/shard_map/ppermute | solution.py:39
  81.5 5.8 %collective-permute-start.17 = (bf16[128,256]{1,0:T(8,128)(2,1)S(1)}, bf16[128,256]{1,0:T(8,128)(2,1)S(1)}, u32[]{:S(2)}, u32[]{:S(2)}) collective-permute-start(bf16[128,256]{1,0:T(8,128)(2,1)S(1)} %get-tuple-element.40), channel_id=1, source_target_pairs={{0,8},{8,16},{16,24},{24,0},{1,9},{9,17},{17,25},{25,1},{2,10},{10... | collective-permute-start | bytes 196616 | tf_op jit(solution)/shard_map/ppermute | solution.py:39
  83.1 6.6 %collective-permute-start.18 = (bf16[128,256]{1,0:T(8,128)(2,1)S(1)}, bf16[128,256]{1,0:T(8,128)(2,1)S(1)}, u32[]{:S(2)}, u32[]{:S(2)}) collective-permute-start(bf16[128,256]{1,0:T(8,128)(2,1)S(1)} %get-tuple-element.41), channel_id=1, source_target_pairs={{0,24},{8,0},{16,8},{24,16},{1,25},{9,1},{17,9},{25,17},{2,26},{10... | collective-permute-start | bytes 196616 | tf_op jit(solution)/shard_map/ppermute | solution.py:39
  87.3 14.8 %collective-permute-start.8 = (bf16[4,256,512]{2,1,0:T(8,128)(2,1)S(1)}, bf16[4,256,512]{2,1,0:T(8,128)(2,1)S(1)}, u32[]{:S(2)}, u32[]{:S(2)}) collective-permute-start(bf16[4,256,512]{2,1,0:T(8,128)(2,1)S(1)} %pad_maximum_fusion.3), channel_id=1, source_target_pairs={{0,3},{1,0},{2,1},{3,2},{4,7},{5,4},{6,5},{7,6},{32,100},{33,101},... | collective-permute-start | bytes 3145736 | tf_op jit(solution)/shard_map/ppermute | solution.py:39
  89.7 49.0 %collective-permute-start.19 = (bf16[4,256,512]{2,1,0:T(8,128)(2,1)}, bf16[4,256,512]{2,1,0:T(8,128)(2,1)S(1)}, u32[]{:S(2)}, u32[]{:S(2)}) collective-permute-start(bf16[4,256,512]{2,1,0:T(8,128)(2,1)} %pad_maximum_fusion.5), channel_id=1, source_target_pairs={{0,3},{1,0},{2,1},{3,2},{4,7},{5,4},{6,5},{7,6},{32,100},{33,101},... | collective-permute-start | bytes 3145736 | tf_op jit(solution)/shard_map/ppermute | solution.py:39
  90.7 4.5 %copy-start.3 = (bf16[256,4096]{1,0:T(8,128)(2,1)S(1)}, bf16[256,4096]{1,0:T(8,128)(2,1)}, u32[]{:S(2)}) copy-start(bf16[256,4096]{1,0:T(8,128)(2,1)} %copy-done.2) | copy-start | bytes 6291460
  90.7 48.0 %collective-permute-start.21 = (bf16[4,256,512]{2,1,0:T(8,128)(2,1)}, bf16[4,256,512]{2,1,0:T(8,128)(2,1)}, u32[]{:S(2)}, u32[]{:S(2)}) collective-permute-start(bf16[4,256,512]{2,1,0:T(8,128)(2,1)} %pad_maximum_fusion.5), channel_id=1, source_target_pairs={{0,1},{1,2},{2,3},{3,0},{4,5},{5,6},{6,7},{7,4},{32,96},{33,97},{3... | collective-permute-start | bytes 3145736 | tf_op jit(solution)/shard_map/ppermute | solution.py:39
  93.8 24.6 %collective-permute-start.9 = (bf16[4,256,512]{2,1,0:T(8,128)(2,1)S(1)}, bf16[4,256,512]{2,1,0:T(8,128)(2,1)S(1)}, u32[]{:S(2)}, u32[]{:S(2)}) collective-permute-start(bf16[4,256,512]{2,1,0:T(8,128)(2,1)S(1)} %pad_maximum_fusion.2.g0), channel_id=1, source_target_pairs={{0,2},{1,3},{2,0},{3,1},{4,6},{5,7},{6,4},{7,5},{32,36},{33,37},{3... | collective-permute-start | bytes 3145736 | tf_op jit(solution)/shard_map/ppermute | solution.py:39
  96.7 28.4 %copy-start = (bf16[1024,4096]{1,0:T(8,128)(2,1)}, bf16[1024,4096]{1,0:T(8,128)(2,1)S(1)}, u32[]{:S(2)}) copy-start(bf16[1024,4096]{1,0:T(8,128)(2,1)S(1)} %pad_maximum_fusion.w_all) | copy-start | bytes 25165828
  96.7 42.0 %collective-permute-start.20 = (bf16[4,256,512]{2,1,0:T(8,128)(2,1)S(1)}, bf16[4,256,512]{2,1,0:T(8,128)(2,1)}, u32[]{:S(2)}, u32[]{:S(2)}) collective-permute-start(bf16[4,256,512]{2,1,0:T(8,128)(2,1)S(1)} %pad_maximum_fusion.4.g0), channel_id=1, source_target_pairs={{0,2},{1,3},{2,0},{3,1},{4,6},{5,7},{6,4},{7,5},{32,36},{33,37},{3... | collective-permute-start | bytes 3145736 | tf_op jit(solution)/shard_map/ppermute | solution.py:39
  125.1 31.6 %all-to-all-start.2 = ((bf16[64,8,1152]{2,1,0:T(8,128)(2,1)}), bf16[64,8,1152]{2,1,0:T(8,128)(2,1)}, u32[]{:S(2)}, u32[]{:S(2)}) async-start(bf16[64,8,1152]{2,1,0:T(8,128)(2,1)} %bitcast.36), calls=%async_computation.2 | async-start | bytes 2359296 | tf_op jit(solution)/shard_map/all_to_all | solution.py:231
  138.7 3.4 %copy-start.1 = (bf16[1024,4096]{1,0:T(8,128)(2,1)S(1)}, bf16[1024,4096]{1,0:T(8,128)(2,1)}, u32[]{:S(2)}) copy-start(bf16[1024,4096]{1,0:T(8,128)(2,1)} %copy-done) | copy-start | bytes 25165828
  149.8 13.1 %copy-start.9 = (f32[128]{0:T(128)S(1)}, f32[128]{0:T(128)}, u32[]{:S(2)}) copy-start(f32[128]{0:T(128)} %param.11) | copy-start | bytes 1540
  156.7 23.3 %all-to-all-start.3 = ((bf16[64,8,1152]{2,1,0:T(8,128)(2,1)}), bf16[64,8,1152]{2,1,0:T(8,128)(2,1)S(1)}, u32[]{:S(2)}, u32[]{:S(2)}) async-start(bf16[64,8,1152]{2,1,0:T(8,128)(2,1)} %bitcast.48), calls=%async_computation.3 | async-start | bytes 2359296 | tf_op jit(solution)/shard_map/all_to_all | solution.py:231
